TPU v7x, 32 devices: a whole 2x2x4 slice. The times are simulated.
32 devices in a mesh: leaf: 4 (over z), panel: 8 (over y, x, core).
Axes of the slice: x: 2, y: 2, z: 4, core: 2. Of those that a mesh axis runs over, the one named last changes fastest.
Arguments:
- pix_grand: int32 [512, 8], P(None, 'leaf'), may hold values from 0 to 255
- pix_mid: int32 [512, 4], replicated, may hold values from 0 to 255
- pix_root: int32 [512], replicated, may hold values from 0 to 255
- parent: int32 [8], P('leaf'), may hold values from 0 to 3
- emit_grand: float32 [8, 4096, 256], P('leaf', 'panel'), may hold values from -232 to -1
- emit_mid: float32 [4, 4096, 256], P(None, 'panel'), may hold values from -232 to -1
- emit_root: float32 [4096, 256], P('leaf'), may hold values from -12 to -1
- weight_grand: float32 [8, 4096, 4096], P('leaf', None, 'panel'), may hold values from 2.4414063e-05 to 0.00048828125
- root_middle_weight: float32 [4, 4096, 4096], P(None, 'leaf', 'panel'), may hold values from 2.4414063e-05 to 0.00048828125
- prior: float32 [4096], P('leaf'), may hold values from 2.4414063e-05 to 0.00048828125
Outputs:
- loglik: float32 [512], replicated
- flow_grand: float32 [8, 4096, 4096], P('leaf', None, 'panel')
- flow_mid: float32 [4, 4096, 4096], P(None, 'leaf', 'panel')
All inputs are finite; a program needn't handle non-finite values.
Results may differ from a plain program's by a relative error of at most 0.0003.
Values sent between devices are 32-bit elements; how exact they have to be, the bound alone decides.
A program may use at most 192 MiB of HBM per device.

v0:
```python
import jax
import jax.numpy as jnp
from jax import lax
from jax.sharding import PartitionSpec as P


def lookup(lookup_matrix, pixels):
    values = lookup_matrix.shape[-1]
    indicator_vector = (
        jnp.transpose(pixels)[:, None, :] == jnp.arange(values, dtype=jnp.int32)[None, :, None]
    ).astype(jnp.float32)
    return jnp.einsum(
        "ozd,odf->ozf", lookup_matrix, indicator_vector, precision=lax.Precision.HIGHEST
    )


def shards(
    pix_grand,
    pix_mid,
    pix_root,
    parent,
    emit_grand,
    emit_mid,
    emit_root,
    weight_grand,
    root_middle_weight,
    prior,
):
    highest = lax.Precision.HIGHEST
    images = pix_grand.shape[0]
    states = weight_grand.shape[1]
    groups = parent.shape[0]
    middles = root_middle_weight.shape[0]
    values = emit_root.shape[1]
    scale = states * states / images
    nodes = groups * lax.axis_size("leaf") + middles + 1
    a_grand = lookup(emit_grand, pix_grand)
    grand_upper = lax.pmax(jnp.max(a_grand, axis=1), "panel")
    e_grand = jnp.exp(a_grand - grand_upper[:, None, :])
    weights = weight_grand
    s_own = lax.psum_scatter(
        jnp.einsum("gij,gjb->igb", weights, e_grand, precision=highest),
        "panel",
        scatter_dimension=0,
        tiled=True,
    )
    m_own = jnp.log(s_own) + grand_upper[None, :, :]
    parent_hot = (parent[:, None] == jnp.arange(middles, dtype=jnp.int32)[None, :]).astype(
        jnp.float32
    )
    contrib = jnp.einsum("gu,kgb->ukb", parent_hot, m_own, precision=highest)
    child_sum = lax.psum(contrib, "leaf")
    a_mid = lookup(emit_mid, pix_mid) + child_sum
    mid_upper = lax.pmax(jnp.max(a_mid, axis=1), "panel")
    e_mid = jnp.exp(a_mid - mid_upper[:, None, :])
    s_mid = lax.psum(
        jnp.einsum("uij,ujb->uib", root_middle_weight, e_mid, precision=highest), "panel"
    )
    m_mid = jnp.log(s_mid) + mid_upper[:, None, :]
    root_hot = (pix_root[None, :] == jnp.arange(values, dtype=jnp.int32)[:, None]).astype(
        jnp.float32
    )
    scores = (
        jnp.log(prior)[:, None]
        + jnp.dot(emit_root, root_hot, precision=highest)
        + jnp.sum(m_mid, axis=0)
    )
    upper = lax.pmax(jnp.max(scores, axis=0), "leaf")
    expo_root = jnp.exp(scores - upper[None, :])
    total = lax.psum(jnp.sum(expo_root, axis=0), "leaf")
    loglik = (upper + jnp.log(total)) / nodes
    q_root = expo_root / total[None, :]
    t_mid = q_root[None, :, :] / s_mid
    flow_mid = (
        root_middle_weight * jnp.einsum("uib,ujb->uij", t_mid, e_mid, precision=highest) * scale
    )
    q_part = e_mid * jnp.einsum("uij,uib->ujb", root_middle_weight, t_mid, precision=highest)
    q_mid = lax.psum(q_part, "leaf")
    ratio_own = jnp.einsum("gu,ukb->kgb", parent_hot, q_mid, precision=highest) / s_own
    weights = weight_grand
    flow_grand = (
        weights
        * jnp.einsum(
            "igb,gjb->gij",
            lax.all_gather(ratio_own, "panel", axis=0, tiled=True),
            e_grand,
            precision=highest,
        )
        * scale
    )
    return (loglik, flow_grand, flow_mid)


def solution(mesh):
    placed = (
        P(None, "leaf"),
        P(),
        P(),
        P("leaf"),
        P("leaf", "panel", None),
        P(None, "panel", None),
        P("leaf", None),
        P("leaf", None, "panel"),
        P(None, "leaf", "panel"),
        P("leaf"),
    )
    return jax.shard_map(
        shards,
        mesh=mesh,
        in_specs=placed,
        out_specs=(P(), P("leaf", None, "panel"), P(None, "leaf", "panel")),
        check_vma=False,
    )
```

profile of v0, /device:TPU:0, one launch (start us, length us, event | category | flops | bytes accessed | tf_op | source)
XLA Modules:
  0.0 923.0 jit_solution(8678759673897978895)
XLA Ops:
  7.2 0.0 copy-start
  7.2 0.0 reduce-scatter.2.cloned.1.call-start
  7.2 3.8 bitcast_reduce_fusion
  11.1 15.1 %pmax.21 = f32[2,512]{1,0:T(2,128)S(1)} all-reduce(f32[2,512]{1,0:T(2,128)S(1)} %get-tuple-element.3), channel_id=1, replica_groups=mesh['leaf'=4,'panel'=8] {'panel'}, use_global_device_ids=true, to_apply=%region_1.0 | all-reduce | flops 1024 | bytes 8192 | tf_op jit(solution)/shard_map/pmax | solution.py:38
  26.2 57.8 %convolution_bitcast_fusion = f32[4096,2,512]{0,2,1:T(8,128)} fusion(f32[2,4096,512]{2,1,0:T(8,128)} %param.17, f32[2,512,512]{1,2,0:T(8,128)} %get-tuple-element.4, f32[2,512]{1,0:T(2,128)S(1)} %pmax.21), kind=kOutput, calls=%fused_computation.1 | convolution fusion | flops 25770328064 | bytes 35655680 | tf_op jit(solution)/shard_map/gij,gjb->igb/dot_general | solution.py:42
  83.9 0.0 reduce-scatter.2.cloned.1.call-update
  84.0 0.0 copy-start.9
  84.0 0.0 all-reduce.4.cloned.1.call-start
  84.0 115.4 %reduce-scatter.2.cloned.1.call-done = f32[512,2,512]{0,2,1:T(8,128)} async-done(((f32[4096,2,512]{0,2,1:T(8,128)}), f32[512,2,512]{0,2,1:T(8,128)}) %reduce-scatter.2.cloned.1.call-update) | async-done | bytes 2097168 | tf_op jit(solution)/shard_map/reduce_scatter | solution.py:41
  199.5 3.2 log_add_fusion
  202.7 4.1 copy.14
  206.8 0.0 copy-done.9
  206.8 6.4 fusion.19
  213.3 3.3 copy.15
  216.5 0.0 copy-start.6
  216.6 0.0 all-reduce.4.cloned.1.call-update
  216.6 0.0 all-reduce.6.cloned.1.call-start
  216.6 155.0 %all-reduce.4.cloned.1.call-done = f32[4,512,512]{2,1,0:T(8,128)} async-done(((f32[4,512,512]{2,1,0:T(8,128)}), f32[4,512,512]{2,1,0:T(8,128)}) %all-reduce.4.cloned.1.call-update) | async-done | bytes 4194320 | tf_op jit(solution)/shard_map/psum | solution.py:52
  371.7 0.0 copy-done
  371.7 0.0 copy-done.6
  371.7 6.3 fusion.23
  378.0 13.9 %pmax.22 = f32[4,512]{1,0:T(4,128)S(1)} all-reduce(f32[4,512]{1,0:T(4,128)S(1)} %get-tuple-element.5), channel_id=1, replica_groups=mesh['leaf'=4,'panel'=8] {'panel'}, use_global_device_ids=true, to_apply=%region_5.0 | all-reduce | flops 2048 | bytes 16384 | tf_op jit(solution)/shard_map/pmax | solution.py:54
  391.9 32.0 %convolution_bitcast_fusion.1 = f32[4,1024,512]{1,2,0:T(8,128)} fusion(f32[4,1024,512]{2,1,0:T(8,128)} %param.18, f32[4,512,512]{2,1,0:T(8,128)} %get-tuple-element.6, f32[4,512]{1,0:T(4,128)S(1)} %pmax.22), kind=kOutput, calls=%fused_computation.10 | convolution fusion | flops 12885950464 | bytes 20979712 | tf_op jit(solution)/shard_map/uij,ujb->uib/dot_general | solution.py:57
  423.9 0.0 copy-start.7
  423.9 0.0 all-reduce.6.cloned.1.call-update
  423.9 0.0 all-reduce.8.cloned.1.call-start
  424.0 0.6 copy-done.7
  424.6 0.0 copy-start.5
  424.6 0.0 copy-start.8
  424.6 123.3 %all-reduce.6.cloned.1.call-done = f32[4,1024,512]{1,2,0:T(8,128)} async-done(((f32[4,1024,512]{1,2,0:T(8,128)}), f32[4,1024,512]{1,2,0:T(8,128)}) %all-reduce.6.cloned.1.call-update) | async-done | bytes 8388624 | tf_op jit(solution)/shard_map/psum | solution.py:56
  547.9 4.3 add_reduce_fusion
  552.3 0.0 copy-done.5
  552.3 0.0 copy-done.8
  552.3 1.5 fusion.24
  553.7 11.7 %pmax.23 = f32[512]{0:T(512)S(1)} all-reduce(f32[512]{0:T(512)S(1)} %get-tuple-element.7), channel_id=1, replica_groups=mesh['leaf'=4,'panel'=8] {'leaf'}, use_global_device_ids=true, to_apply=%region_9.0 | all-reduce | flops 512 | bytes 4096 | tf_op jit(solution)/shard_map/pmax | solution.py:68
  565.4 0.5 fusion.7
  565.9 8.4 psum.30
  574.3 0.0 copy-start.2
  574.3 0.5 fusion.6
  574.7 0.0 copy-start.4
  574.8 1.3 copy-done.4
  576.0 1.2 copy-done.2
  577.2 19.5 %bitcast_multiply_fusion = f32[4,512,512]{2,1,0:T(8,128)} fusion(f32[4,512,512]{2,1,0:T(8,128)S(1)} %copy-done.2, f32[4,512]{1,0:T(4,128)S(1)} %pmax.22, f32[4,1024,512]{2,1,0:T(8,128)} %param.18, f32[4,1024,512]{1,2,0:T(8,128)} %all-reduce.6.cloned.1.call-done, f32[1024,512]{0,1:T(8,128)S(1)} %fusion.6), kind=kOutput, calls=%fused_computation.4 | convolution fusion | flops 12889096192 | bytes 27271168 | tf_op jit(solution)/shard_map/uij,uib->ujb/dot_general | solution.py:77
  596.8 0.0 all-reduce.8.cloned.1.call-update
  596.8 0.0 copy-start.3
  596.8 0.0 all-gather.2.cloned.1.call-start
  596.8 153.9 %all-reduce.8.cloned.1.call-done = f32[4,512,512]{2,1,0:T(8,128)} async-done(((f32[4,512,512]{2,1,0:T(8,128)}), f32[4,512,512]{2,1,0:T(8,128)}) %all-reduce.8.cloned.1.call-update) | async-done | bytes 4194320 | tf_op jit(solution)/shard_map/psum | solution.py:78
  750.8 9.8 %fusion = f32[512,512,2]{1,2,0:T(2,128)} fusion(f32[4,512,512]{2,1,0:T(8,128)} %all-reduce.8.cloned.1.call-done, s32[2]{0:T(128)S(1)} %copy-done.9), kind=kOutput, calls=%fused_computation.6 | convolution fusion | flops 25165832 | bytes 6291464 | tf_op jit(solution)/shard_map/gu,ukb->kgb/dot_general | solution.py:79
  760.6 4.1 copy.22
  764.7 0.0 copy-done.3
  764.7 3.4 bitcast_divide_fusion
  768.2 0.0 all-gather.2.cloned.1.call-update
  768.2 0.6 add_multiply_fusion
  768.8 34.6 %multiply_multiply_fusion.1 = f32[4,1024,512]{2,1,0:T(8,128)} fusion(f32[4,1024,512]{2,1,0:T(8,128)} %param.18, f32[4,512,512]{2,1,0:T(8,128)} %get-tuple-element.6, f32[4,1024,512]{1,2,0:T(8,128)} %all-reduce.6.cloned.1.call-done, f32[1024,512]{0,1:T(8,128)} %copy-done.4, f32[4,512]{1,0:T(4,128)S(1)} %pmax.22), kind=kOutput, calls=%fused_computation.2 | convolution fusion | flops 12892241920 | bytes 31465472 | tf_op jit(solution)/shard_map/uib,ujb->uij/dot_general | solution.py:75
  803.4 53.8 %all-gather.2.cloned.1.call-done = f32[4096,2,512]{0,2,1:T(8,128)} async-done(((f32[512,2,512]{0,2,1:T(8,128)}), f32[4096,2,512]{0,2,1:T(8,128)}) %all-gather.2.cloned.1.call-update) | async-done | bytes 16777232 | tf_op jit(solution)/shard_map/all_gather | solution.py:85
  857.2 0.0 copy-start.1
  857.2 59.0 %multiply_multiply_fusion = f32[2,4096,512]{2,1,0:T(8,128)} fusion(f32[2,4096,512]{2,1,0:T(8,128)} %param.17, f32[4096,2,512]{0,2,1:T(8,128)} %all-gather.2.cloned.1.call-done, f32[2,512,512]{1,2,0:T(8,128)} %get-tuple-element.4, f32[2,512]{1,0:T(2,128)S(1)} %pmax.21), kind=kOutput, calls=%fused_computation | convolution fusion | flops 25778716672 | bytes 52432896 | tf_op jit(solution)/shard_map/igb,gjb->gij/dot_general | solution.py:83
  916.2 0.0 copy-done.1
  (1 shorter events, 0.0 us)
Async XLA Ops:
  7.2 364.5 %copy-start = (f32[4,512,256]{2,1,0:T(8,128)S(1)}, f32[4,512,256]{2,1,0:T(8,128)}, u32[]{:S(2)}) copy-start(f32[4,512,256]{2,1,0:T(8,128)} %param.15) | copy-start | bytes 6291460
  7.2 192.3 %reduce-scatter.2.cloned.1.call-start = ((), (), s32[]{:S(2)}) async-start(), calls=%async_computation.1 | async-start | bytes 18874368 | tf_op jit(solution)/shard_map/reduce_scatter | solution.py:41
  84.0 122.8 %copy-start.9 = (s32[2]{0:T(128)S(1)}, s32[2]{0:T(128)}, u32[]{:S(2)}) copy-start(s32[2]{0:T(128)} %param.13) | copy-start | bytes 28
  84.0 287.7 %all-reduce.4.cloned.1.call-start = ((), (), s32[]{:S(2)}) async-start(), calls=%async_computation.2 | async-start | bytes 8388608 | tf_op jit(solution)/shard_map/psum | solution.py:52
  216.5 155.1 %copy-start.6 = (s32[512,4]{0,1:T(4,128)S(1)}, s32[512,4]{0,1:T(4,128)}, u32[]{:S(2)}) copy-start(s32[512,4]{0,1:T(4,128)} %param.11) | copy-start | bytes 24580
  216.6 331.4 %all-reduce.6.cloned.1.call-start = ((), (), s32[]{:S(2)}) async-start(), calls=%async_computation.3 | async-start | bytes 16777216 | tf_op jit(solution)/shard_map/psum | solution.py:56
  423.9 0.7 copy-start.7
  423.9 326.8 %all-reduce.8.cloned.1.call-start = ((), (), s32[]{:S(2)}) async-start(), calls=%async_computation.4 | async-start | bytes 8388608 | tf_op jit(solution)/shard_map/psum | solution.py:78
  424.6 127.7 %copy-start.5 = (f32[1024,256]{1,0:T(8,128)S(1)}, f32[1024,256]{1,0:T(8,128)}, u32[]{:S(2)}) copy-start(f32[1024,256]{1,0:T(8,128)} %param.16) | copy-start | bytes 3145732
  424.6 127.7 %copy-start.8 = (s32[512]{0:T(512)S(1)}, s32[512]{0:T(512)}, u32[]{:S(2)}) copy-start(s32[512]{0:T(512)} %param.12) | copy-start | bytes 6148
  574.3 2.9 copy-start.2
  574.7 1.3 copy-start.4
  596.8 167.9 %copy-start.3 = (f32[512,2,512]{0,2,1:T(8,128)S(1)}, f32[512,2,512]{0,2,1:T(8,128)}, u32[]{:S(2)}) copy-start(f32[512,2,512]{0,2,1:T(8,128)} %reduce-scatter.2.cloned.1.call-done) | copy-start | bytes 6291460
  596.8 260.4 %all-gather.2.cloned.1.call-start = ((), (), s32[]{:S(2)}) async-start(), calls=%async_computation.5 | async-start | bytes 18874368 | tf_op jit(solution)/shard_map/all_gather | solution.py:85
  857.2 59.0 %copy-start.1 = (f32[4,512,256]{2,1,0:T(8,128)S(1)}, f32[4,512,256]{2,1,0:T(8,128)}, u32[]{:S(2)}) copy-start(f32[4,512,256]{2,1,0:T(8,128)} %param.15) | copy-start | bytes 6291460
Sparse Core Ops, SparseCore 0:
  84.1 115.3 reduce-scatter.1
  216.7 154.9 all-reduce.3
  424.0 123.8 all-reduce.5
  596.9 153.8 all-reduce.7
  768.3 88.8 all-gather.1
where the time goes:
time: 934 us; the launch traced here: 923 us
  waiting for transfers between devices  602 us (64%)
  matrix products  231 us (25%)
  blocking collectives  49 us (5%)
  local copies, waits for them, and re-layouts  14.6 us (2%)
  between operations  14.1 us (2%)
  other arithmetic  12.5 us (1%)
    psum x1, waiting for transfers between devices, shards(): child_sum = lax.psum(contrib, 'leaf')  155 us
    psum x1, waiting for transfers between devices, shards(): q_mid = lax.psum(q_part, 'leaf')  154 us
    psum x1, waiting for transfers between devices, shards(): lax.psum(jnp.einsum('uij,ujb->uib', root_middle_weight, e_mid, precision=...  123 us
    reduce_scatter x1, waiting for transfers between devices, shards(): lax.psum_scatter(jnp.einsum('gij,gjb->igb', weights, e_grand, precision=h...  115 us
    dot_general x1, matrix products, shards(): jnp.einsum('igb,gjb->gij', lax.all_gather(ratio_own, 'panel', axis=0, til...  59 us
    dot_general x1, matrix products, shards(): jnp.einsum('gij,gjb->igb', weights, e_grand, precision=highest)  57.8 us
    all_gather x1, waiting for transfers between devices, shards(): lax.all_gather(ratio_own, 'panel', axis=0, tiled=True)  53.8 us
    dot_general x1, matrix products, shards(): jnp.einsum('uib,ujb->uij', t_mid, e_mid, precision=highest)  34.6 us
  transfers between devices with their start and end apart: 5, of which 5 were waited for; matrix products, arithmetic and copies ran while one was open for 4% of the time, Pallas kernels for 0%

commit v1 on v0

v1 whole, which is shorter than its diff:
```python
import jax
import jax.numpy as jnp
from jax import lax
from jax.sharding import PartitionSpec as P

CHUNKS = 2


def one_hot(pixels, values):
    return (pixels[..., None, :] == jnp.arange(values, dtype=jnp.int32)[:, None]).astype(
        jnp.float32
    )


def lookup(lookup_matrix, pixels):
    return jnp.einsum(
        "ozd,odf->ozf",
        lookup_matrix,
        one_hot(jnp.transpose(pixels), lookup_matrix.shape[-1]),
        precision=lax.Precision.HIGHEST,
    )


def inward(total, axis, step):
    size = lax.axis_size(axis)
    if size % 2 or step >= size // 2 - 1:
        return total
    pairs = [(step, step + 1), (size - 1 - step, size - 2 - step)]
    return total + lax.ppermute(total, axis, pairs)


def across(total, axis):
    size = lax.axis_size(axis)
    if size % 2:
        return lax.psum(total, axis)
    half = size // 2
    for step in range(1, half - 1):
        total = inward(total, axis, step)
    return total + lax.ppermute(total, axis, [(half - 1, half), (half, half - 1)])


def outward(total, axis):
    size = lax.axis_size(axis)
    if size % 2:
        return total
    me = lax.axis_index(axis)
    for source in range(size // 2 - 1, 0, -1):
        pairs = [(source, source - 1), (size - 1 - source, size - source)]
        received = lax.ppermute(total, axis, pairs)
        total = jnp.where((me == source - 1) | (me == size - source), received, total)
    return total


def shards(
    pix_grand,
    pix_mid,
    pix_root,
    parent,
    emit_grand,
    emit_mid,
    emit_root,
    weight_grand,
    root_middle_weight,
    prior,
):
    high = lax.Precision.HIGH
    highest = lax.Precision.HIGHEST
    images = pix_grand.shape[0]
    states = weight_grand.shape[1]
    groups = parent.shape[0]
    middles = root_middle_weight.shape[0]
    leaves, panels = lax.axis_size("leaf"), lax.axis_size("panel")
    my_leaf, my_panel = lax.axis_index("leaf"), lax.axis_index("panel")
    scale = states * states / images
    nodes = groups * leaves + middles + 1
    width = images // CHUNKS
    rows = emit_root.shape[0] // panels

    a_grand = lookup(emit_grand, pix_grand)
    grand_upper = jnp.max(lax.all_gather(jnp.max(a_grand, axis=1), "panel"), axis=0)
    a_mid_own = lookup(emit_mid, pix_mid)
    e_grand = jnp.exp(a_grand - grand_upper[:, None, :])
    own_emit = lax.dynamic_slice_in_dim(emit_root, my_panel * rows, rows, 0)
    own_prior = lax.dynamic_slice_in_dim(prior, my_panel * rows, rows, 0)
    root_own = jnp.log(own_prior)[:, None] + jnp.dot(
        own_emit, one_hot(pix_root, emit_root.shape[1]), precision=highest
    )

    spans = [slice(chunk * width, (chunk + 1) * width) for chunk in range(CHUNKS)]
    s_all = [
        [
            lax.psum_scatter(
                jnp.dot(weight_grand[g], e_grand[g, :, here], precision=high),
                "panel",
                scatter_dimension=0,
                tiled=True,
            )
            for g in range(groups)
        ]
        for here in spans
    ]

    def children(s_own, here):
        m_own = [jnp.log(s_own[g]) + grand_upper[g, None, here] for g in range(groups)]
        return [
            inward(sum(jnp.where(parent[g] == u, m_own[g], 0.0) for g in range(groups)), "leaf", 0)
            for u in range(middles)
        ]

    logliks, mid_flows, grand_flows = [], [], []
    child = [outward(across(begun, "leaf"), "leaf") for begun in children(s_all[0], spans[0])]
    ratio_before, q_begun = None, []

    def divided(begun, chunk):
        q_mid = [outward(value, "leaf") for value in begun]
        return jnp.stack(
            [
                sum(jnp.where(parent[g] == u, q_mid[u], 0.0) for u in range(middles))
                / s_all[chunk][g]
                for g in range(groups)
            ],
            axis=1,
        )

    def collect(ratio_own, here):
        t_grand = lax.all_gather(ratio_own, "panel", axis=0, tiled=True)
        grand_flows.append(
            jnp.einsum("igb,gjb->gij", t_grand, e_grand[:, :, here], precision=high)
        )

    for chunk, here in enumerate(spans):
        a_mid = jnp.stack([a_mid_own[u, :, here] + child[u] for u in range(middles)])
        mid_local = jnp.max(a_mid, axis=1)
        e_local = jnp.exp(a_mid - mid_local[:, None, :])
        partial = jnp.einsum("uij,ujb->iub", root_middle_weight, e_local, precision=high)
        mid_upper = jnp.max(lax.all_gather(mid_local, "panel"), axis=0)
        begun = []
        if chunk + 1 < CHUNKS:
            s_all[chunk + 1], mid_local = lax.optimization_barrier((s_all[chunk + 1], mid_local))
            begun = children(s_all[chunk + 1], spans[chunk + 1])
        partial, begun[:1], q_begun[:1] = lax.optimization_barrier(
            (partial, begun[:1], q_begun[:1])
        )
        begun = [across(value, "leaf") for value in begun]
        q_begun = [across(value, "leaf") for value in q_begun]
        shift = jnp.exp(mid_local - mid_upper)
        e_mid = e_local * shift[:, None, :]
        s_mid = lax.psum_scatter(
            partial * shift[None], "panel", scatter_dimension=0, tiled=True
        )
        s_mid, begun, q_begun = lax.optimization_barrier((s_mid, begun, q_begun))
        child = [outward(value, "leaf") for value in begun]
        ratio_before = divided(q_begun, chunk - 1) if chunk else None
        scores = root_own[:, here] + jnp.sum(jnp.log(s_mid) + mid_upper[None], axis=1)
        root_local = jnp.max(scores, axis=0)
        expo_root = jnp.exp(scores - root_local[None, :])
        stats = lax.all_gather(
            jnp.stack([root_local, jnp.sum(expo_root, axis=0)]), ("leaf", "panel")
        )
        t_rows = lax.all_gather(expo_root[:, None, :] / s_mid, "panel", axis=0)
        if ratio_before is not None:
            t_rows, ratio_before = lax.optimization_barrier((t_rows, ratio_before))
            collect(ratio_before, spans[chunk - 1])
        upper = jnp.max(stats[:, 0], axis=0)
        total = jnp.sum(stats[:, 1] * jnp.exp(stats[:, 0] - upper[None]), axis=0)
        logliks.append((upper + jnp.log(total)) / nodes)
        block = lax.dynamic_slice_in_dim(stats[:, 0], my_leaf * panels, panels, 0)
        share = jnp.exp(block - upper[None]) / total[None]
        t_mid = (t_rows * share[:, None, None, :]).reshape(panels * rows, middles, width)
        q_part = e_mid * jnp.einsum("uij,iub->ujb", root_middle_weight, t_mid, precision=high)
        if chunk + 1 < CHUNKS:
            child, q_part = lax.optimization_barrier((child, q_part))
        q_begun = [inward(q_part[u], "leaf", 0) for u in range(middles)]
        mid_flows.append(jnp.einsum("iub,ujb->uij", t_mid, e_mid, precision=high))
    q_begun = [across(value, "leaf") for value in q_begun]
    collect(divided(q_begun, CHUNKS - 1), spans[-1])
    return (
        jnp.concatenate(logliks),
        weight_grand * sum(grand_flows) * scale,
        root_middle_weight * sum(mid_flows) * scale,
    )


def solution(mesh):
    placed = (
        P(None, "leaf"),
        P(),
        P(),
        P("leaf"),
        P("leaf", "panel", None),
        P(None, "panel", None),
        P("leaf", None),
        P("leaf", None, "panel"),
        P(None, "leaf", "panel"),
        P("leaf"),
    )
    return jax.shard_map(
        shards,
        mesh=mesh,
        in_specs=placed,
        out_specs=(P(), P("leaf", None, "panel"), P(None, "leaf", "panel")),
        check_vma=False,
    )
```

time: 934 us -> 887 us (0.950)
  waiting for transfers between devices: 602 us -> 410 us
  blocking collectives: 49 us -> 144 us
  matrix products: 231 us -> 140 us
  starting transfers between devices: 0.21 us -> 66 us
  other arithmetic: 12.5 us -> 63.4 us
  local copies, waits for them, and re-layouts: 14.6 us -> 32.8 us
    psum x3 -> x0, waiting for transfers between devices: 432 us -> none  [the longest x1 155 us: shards(): child_sum = lax.psum(contrib, 'leaf')]
    ppermute x0 -> x48, waiting for transfers between devices: none -> 266 us  [the longest x16 141 us: outward(): received = lax.ppermute(total, axis, pairs)]
    all_gather x0 -> x5, blocking collectives: none -> 144 us  [the longest x2 118 us: shards(): lax.all_gather(jnp.stack([root_local, jnp.sum(expo_root, axis=0)]), ('lea...]
    dot_general x10 -> x15, matrix products: 231 us -> 140 us  [the longest x4 36.7 us: shards(): jnp.dot(weight_grand[g], e_grand[g, :, here], precision=high)]
    ppermute x0 -> x48, starting transfers between devices: none -> 65.4 us  [the longest x16 29.4 us: inward(): return total + lax.ppermute(total, axis, pairs)]
    pmax x3 -> x0, blocking collectives: 40.7 us -> none  [the longest x1 15.1 us: shards(): grand_upper = lax.pmax(jnp.max(a_grand, axis=1), 'panel')]
    all_gather x1 -> x4, waiting for transfers between devices: 53.8 us -> 19.6 us  [the longest x2 19.6 us: collect(): t_grand = lax.all_gather(ratio_own, 'panel', axis=0, tiled=True)]
    add x1 -> x28, other arithmetic: 3.22 us -> 23.6 us  [the longest x16 12.3 us: across(): total + lax.ppermute(total, axis, [(half - 1, half), (half, half - 1)])]
  transfers between devices with their start and end apart: 5 -> 58, of which waited for: 5 -> 31; matrix products, arithmetic and copies ran while one was open for 4% -> 16% of each run, Pallas kernels for 0% -> 0%
where the time goes in v1:
time: 887 us; the launch traced here: 878 us
  waiting for transfers between devices  410 us (46%)
  blocking collectives  144 us (16%)
  matrix products  140 us (16%)
  starting transfers between devices  66 us (7%)
  other arithmetic  63.4 us (7%)
  local copies, waits for them, and re-layouts  32.8 us (4%)
  between operations  21 us (2%)
    ppermute x16, waiting for transfers between devices, outward(): received = lax.ppermute(total, axis, pairs)  141 us
    ppermute x16, waiting for transfers between devices, inward(): return total + lax.ppermute(total, axis, pairs)  125 us
    all_gather x2, blocking collectives, shards(): lax.all_gather(jnp.stack([root_local, jnp.sum(expo_root, axis=0)]), ('lea...  118 us
    reduce_scatter x4, waiting for transfers between devices, shards(): lax.psum_scatter(jnp.dot(weight_grand[g], e_grand[g, :, here], precision=...  78.8 us
    reduce_scatter x2, waiting for transfers between devices, shards(): lax.psum_scatter(partial * shift[None], 'panel', scatter_dimension=0, til...  45.7 us
    dot_general x4, matrix products, shards(): jnp.dot(weight_grand[g], e_grand[g, :, here], precision=high)  36.7 us
    dot_general x2, matrix products, collect(): jnp.einsum('igb,gjb->gij', t_grand, e_grand[:, :, here], precision=high)  35.2 us
    ppermute x16, starting transfers between devices, inward(): return total + lax.ppermute(total, axis, pairs)  29.4 us
  transfers between devices with their start and end apart: 58, of which 31 were waited for; matrix products, arithmetic and copies ran while one was open for 16% of the time, Pallas kernels for 0%

profile of v1, /device:TPU:0, one launch (start us, length us, event | category | flops | bytes accessed | tf_op | source)
XLA Modules:
  0.0 877.9 jit_solution(12843104304693938365)
XLA Ops:
  7.2 3.8 bitcast_reduce_fusion
  11.0 10.5 %all-gather.7 = f32[8,2,512]{2,1,0:T(2,128)S(1)} all-gather(f32[1,2,512]{2,1,0:T(2,128)S(1)} %bitcast.254), channel_id=2, replica_groups=mesh['leaf'=4,'panel'=8] {'panel'}, dimensions={0}, use_global_device_ids=true | all-gather | bytes 36864 | tf_op jit(solution)/shard_map/all_gather | solution.py:80
  24.8 8.8 %fusion.12 = f32[4096,256]{1,0:T(8,128)} fusion(f32[2,4096,512]{2,1,0:T(8,128)} %param.17, f32[2,512,512]{2,1,0:T(8,128)S(1)} %fusion.24), kind=kOutput, calls=%fused_computation.14 | convolution fusion | flops 3221225472 | bytes 13107200 | tf_op jit(solution)/shard_map/dot_general | solution.py:93
  33.7 9.0 %fusion.18 = f32[4096,256]{1,0:T(8,128)} fusion(f32[2,4096,512]{2,1,0:T(8,128)} %param.17, f32[2,512,512]{2,1,0:T(8,128)} %copy-done.3), kind=kOutput, calls=%fused_computation.16 | convolution fusion | flops 3221225472 | bytes 13107200 | tf_op jit(solution)/shard_map/dot_general | solution.py:93
  42.9 9.9 %fusion.15 = f32[4096,256]{1,0:T(8,128)} fusion(f32[2,4096,512]{2,1,0:T(8,128)} %param.17, f32[2,512,512]{2,1,0:T(8,128)} %copy-done.3), kind=kOutput, calls=%fused_computation.15 | convolution fusion | flops 3221225472 | bytes 13107200 | tf_op jit(solution)/shard_map/dot_general | solution.py:93
  52.9 9.0 %fusion.21 = f32[4096,256]{1,0:T(8,128)} fusion(f32[2,4096,512]{2,1,0:T(8,128)} %param.17, f32[2,512,512]{2,1,0:T(8,128)} %copy-done.3), kind=kOutput, calls=%fused_computation.17 | convolution fusion | flops 3221225472 | bytes 13107200 | tf_op jit(solution)/shard_map/dot_general | solution.py:93
  68.3 17.1 %reduce-scatter.7.cloned.1.call-done = f32[512,256]{1,0:T(8,128)} async-done(((f32[4096,256]{1,0:T(8,128)}), f32[512,256]{1,0:T(8,128)}) %reduce-scatter.7.cloned.1.call-update) | async-done | bytes 524304 | tf_op jit(solution)/shard_map/reduce_scatter | solution.py:92
  85.4 55.1 %reduce-scatter.9.cloned.1.call-done = f32[512,256]{1,0:T(8,128)} async-done(((f32[4096,256]{1,0:T(8,128)}), f32[512,256]{1,0:T(8,128)}) %reduce-scatter.9.cloned.1.call-update) | async-done | bytes 524304 | tf_op jit(solution)/shard_map/reduce_scatter | solution.py:92
  142.1 3.4 collective-permute-start
  149.5 8.3 collective-permute-done
  158.5 10.5 %collective-permute-done.9 = f32[512,256]{1,0:T(8,128)S(1)} collective-permute-done((f32[512,256]{1,0:T(8,128)S(1)}, f32[512,256]{1,0:T(8,128)S(1)}, u32[]{:S(2)}, u32[]{:S(2)}) %collective-permute-start.9) | collective-permute-done | bytes 524320 | tf_op jit(solution)/shard_map/ppermute | solution.py:29
  169.8 10.5 %collective-permute-done.6 = f32[512,256]{1,0:T(8,128)S(1)} collective-permute-done((f32[512,256]{1,0:T(8,128)S(1)}, f32[512,256]{1,0:T(8,128)S(1)}, u32[]{:S(2)}, u32[]{:S(2)}) %collective-permute-start.6) | collective-permute-done | bytes 524320 | tf_op jit(solution)/shard_map/ppermute | solution.py:29
  181.0 9.3 %collective-permute-done.3 = f32[512,256]{1,0:T(8,128)S(1)} collective-permute-done((f32[512,256]{1,0:T(8,128)S(1)}, f32[512,256]{1,0:T(8,128)S(1)}, u32[]{:S(2)}, u32[]{:S(2)}) %collective-permute-start.3) | collective-permute-done | bytes 524320 | tf_op jit(solution)/shard_map/ppermute | solution.py:29
  200.7 10.1 %collective-permute-done.2 = f32[512,256]{1,0:T(8,128)} collective-permute-done((f32[512,256]{1,0:T(8,128)S(1)}, f32[512,256]{1,0:T(8,128)}, u32[]{:S(2)}, u32[]{:S(2)}) %collective-permute-start.2) | collective-permute-done | bytes 524320 | tf_op jit(solution)/shard_map/ppermute | solution.py:49
  210.8 11.2 %collective-permute-done.11 = f32[512,256]{1,0:T(8,128)} collective-permute-done((f32[512,256]{1,0:T(8,128)S(1)}, f32[512,256]{1,0:T(8,128)}, u32[]{:S(2)}, u32[]{:S(2)}) %collective-permute-start.11) | collective-permute-done | bytes 524320 | tf_op jit(solution)/shard_map/ppermute | solution.py:49
  222.0 11.2 %collective-permute-done.8 = f32[512,256]{1,0:T(8,128)} collective-permute-done((f32[512,256]{1,0:T(8,128)}, f32[512,256]{1,0:T(8,128)}, u32[]{:S(2)}, u32[]{:S(2)}) %collective-permute-start.8) | collective-permute-done | bytes 524320 | tf_op jit(solution)/shard_map/ppermute | solution.py:49
  233.2 9.3 %collective-permute-done.5 = f32[512,256]{1,0:T(8,128)} collective-permute-done((f32[512,256]{1,0:T(8,128)}, f32[512,256]{1,0:T(8,128)}, u32[]{:S(2)}, u32[]{:S(2)}) %collective-permute-start.5) | collective-permute-done | bytes 524320 | tf_op jit(solution)/shard_map/ppermute | solution.py:49
  244.7 6.6 reduce-scatter.13.cloned.1.call-done
  251.3 2.5 select_add_fusion
  253.8 4.2 collective-permute-start.12
  258.0 9.0 %all-gather.8 = f32[8,4,256]{2,1,0:T(4,128)S(1)} all-gather(f32[1,4,256]{2,1,0:T(4,128)S(1)} %bitcast.252), channel_id=3, replica_groups=mesh['leaf'=4,'panel'=8] {'panel'}, dimensions={0}, use_global_device_ids=true | all-gather | bytes 36864 | tf_op jit(solution)/shard_map/all_gather | solution.py:136
  267.1 9.5 %convolution_bitcast_fusion.1 = f32[1024,4,256]{0,2,1:T(8,128)S(1)} fusion(f32[4,1024,512]{2,1,0:T(8,128)} %param.18, f32[4,256]{1,0:T(4,128)S(1)} %fusion.80, f32[1,512,256]{2,1,0:T(8,128)S(1)} %get-tuple-element.64, f32[1,512,256]{2,1,0:T(8,128)S(1)} %get-tuple-element.65, f32[1,512,256]{2,1,0:T(8,128)S(1)} %get-tuple-element.66, ...), kind=kOutput, calls=%fused_computation.19 | convolution fusion | flops 3223322624 | bytes 14684160 | tf_op jit(solution)/shard_map/uij,ujb->iub/dot_general | solution.py:135
  277.8 2.4 broadcast_multiply_fusion.3
  286.9 7.9 collective-permute-done.14
  297.3 8.6 collective-permute-done.16
  308.5 8.4 collective-permute-done.18
  328.3 2.5 reduce-scatter.15.cloned.1.call-done
  342.6 76.1 %all-gather.9 = f32[32,2,256]{2,1,0:T(2,128)S(1)} all-gather(f32[1,2,256]{2,1,0:T(2,128)S(1)} %maximum_bitcast_fusion), channel_id=4, replica_groups=mesh['leaf'=4,'panel'=8] {'leaf','panel'}, dimensions={0}, use_global_device_ids=true | all-gather | bytes 67584 | tf_op jit(solution)/shard_map/all_gather | solution.py:157
  428.6 3.2 copy.99
  431.8 2.4 broadcast_multiply_fusion.2
  434.2 5.2 copy.71
  439.5 11.6 %bitcast_multiply_fusion.1 = f32[4,512,256]{2,1,0:T(8,128)S(1)} fusion(f32[1024,4,256]{2,0,1:T(8,128)} %bitcast.244, f32[4,1024,512]{2,1,0:T(8,128)} %param.18, f32[4,256]{1,0:T(4,128)S(1)} %subtract_exponential_fusion.9, f32[4,256]{1,0:T(4,128)S(1)} %fusion.80, f32[1,512,256]{2,1,0:T(8,128)S(1)} %get-tuple-element.64, f32[1,512,256]{2,1,0:T(8,128)} %copy-done.15, ...), kind=kOutput, calls=%fused_computation.24 | convolution fusion | flops 3224371200 | bytes 16785408 | tf_op jit(solution)/shard_map/uij,iub->ujb/dot_general | solution.py:170
  452.5 2.2 collective-permute-start.30
  454.7 2.1 collective-permute-start.28
  456.8 2.1 collective-permute-start.26
  462.5 7.4 all-gather.10
  469.9 10.3 %convolution_bitcast_fusion = f32[1024,4,256]{0,2,1:T(8,128)S(1)} fusion(f32[4,1024,512]{2,1,0:T(8,128)} %param.18, f32[4,256]{1,0:T(4,128)S(1)} %fusion.79, f32[1,512,256]{2,1,0:T(8,128)S(1)} %get-tuple-element.60, f32[1,512,256]{2,1,0:T(8,128)} %copy-done.7, f32[1,512,256]{2,1,0:T(8,128)} %copy-done.9, f32[1,512,256]{2,1,0:T(8,128)S(1)} %get-tuple-element.59), kind=kOutput, calls=%fused_computation.18 | convolution fusion | flops 3223322624 | bytes 14684160 | tf_op jit(solution)/shard_map/uij,ujb->iub/dot_general | solution.py:135
  480.2 8.7 collective-permute-done.26
  488.9 11.0 %collective-permute-done.24 = f32[512,256]{1,0:T(8,128)} collective-permute-done((f32[512,256]{1,0:T(8,128)}, f32[512,256]{1,0:T(8,128)}, u32[]{:S(2)}, u32[]{:S(2)}) %collective-permute-start.24) | collective-permute-done | bytes 524320 | tf_op jit(solution)/shard_map/ppermute | solution.py:29
  499.9 2.9 fusion.74
  502.8 2.4 broadcast_multiply_fusion.1
  511.8 43.2 %reduce-scatter.17.cloned.1.call-done = f32[128,4,256]{0,2,1:T(8,128)} async-done(((f32[1024,4,256]{0,2,1:T(8,128)}), f32[128,4,256]{0,2,1:T(8,128)}) %reduce-scatter.17.cloned.1.call-update) | async-done | bytes 524304 | tf_op jit(solution)/shard_map/reduce_scatter | solution.py:148
  567.3 12.2 %collective-permute-done.32 = f32[512,256]{1,0:T(8,128)S(1)} collective-permute-done((f32[512,256]{1,0:T(8,128)S(1)}, f32[512,256]{1,0:T(8,128)S(1)}, u32[]{:S(2)}, u32[]{:S(2)}) %collective-permute-start.32) | collective-permute-done | bytes 524320 | tf_op jit(solution)/shard_map/ppermute | solution.py:49
  579.5 11.2 %collective-permute-done.33 = f32[512,256]{1,0:T(8,128)S(1)} collective-permute-done((f32[512,256]{1,0:T(8,128)S(1)}, f32[512,256]{1,0:T(8,128)S(1)}, u32[]{:S(2)}, u32[]{:S(2)}) %collective-permute-start.33) | collective-permute-done | bytes 524320 | tf_op jit(solution)/shard_map/ppermute | solution.py:49
  590.7 11.2 %collective-permute-done.34 = f32[512,256]{1,0:T(8,128)S(1)} collective-permute-done((f32[512,256]{1,0:T(8,128)S(1)}, f32[512,256]{1,0:T(8,128)S(1)}, u32[]{:S(2)}, u32[]{:S(2)}) %collective-permute-start.34) | collective-permute-done | bytes 524320 | tf_op jit(solution)/shard_map/ppermute | solution.py:49
  602.0 9.5 %collective-permute-done.35 = f32[512,256]{1,0:T(8,128)S(1)} collective-permute-done((f32[512,256]{1,0:T(8,128)S(1)}, f32[512,256]{1,0:T(8,128)S(1)}, u32[]{:S(2)}, u32[]{:S(2)}) %collective-permute-start.35) | collective-permute-done | bytes 524320 | tf_op jit(solution)/shard_map/ppermute | solution.py:49
  614.3 5.2 copy.100
  619.7 41.5 %all-gather.11 = f32[32,2,256]{2,1,0:T(2,128)S(1)} all-gather(f32[1,2,256]{2,1,0:T(2,128)S(1)} %maximum_bitcast_fusion.1), channel_id=7, replica_groups=mesh['leaf'=4,'panel'=8] {'leaf','panel'}, dimensions={0}, use_global_device_ids=true | all-gather | bytes 67584 | tf_op jit(solution)/shard_map/all_gather | solution.py:157
  661.4 4.7 broadcast_multiply_fusion
  666.1 5.2 copy.80
  671.4 11.6 %bitcast_multiply_fusion = f32[4,512,256]{2,1,0:T(8,128)S(1)} fusion(f32[1024,4,256]{2,0,1:T(8,128)} %bitcast.246, f32[4,1024,512]{2,1,0:T(8,128)} %param.18, f32[4,256]{1,0:T(4,128)S(1)} %subtract_exponential_fusion.8, f32[4,256]{1,0:T(4,128)S(1)} %fusion.79, f32[1,512,256]{2,1,0:T(8,128)S(1)} %get-tuple-element.60, f32[1,512,256]{2,1,0:T(8,128)} %copy-done.7, ...), kind=kOutput, calls=%fused_computation.23 | convolution fusion | flops 3224371200 | bytes 16785408 | tf_op jit(solution)/shard_map/uij,iub->ujb/dot_general | solution.py:170
  688.5 8.2 collective-permute-done.45
  696.7 11.2 %collective-permute-done.42 = f32[512,256]{1,0:T(8,128)S(1)} collective-permute-done((f32[512,256]{1,0:T(8,128)S(1)}, f32[512,256]{1,0:T(8,128)S(1)}, u32[]{:S(2)}, u32[]{:S(2)}) %collective-permute-start.42) | collective-permute-done | bytes 524320 | tf_op jit(solution)/shard_map/ppermute | solution.py:29
  707.9 11.2 %collective-permute-done.39 = f32[512,256]{1,0:T(8,128)S(1)} collective-permute-done((f32[512,256]{1,0:T(8,128)S(1)}, f32[512,256]{1,0:T(8,128)S(1)}, u32[]{:S(2)}, u32[]{:S(2)}) %collective-permute-start.39) | collective-permute-done | bytes 524320 | tf_op jit(solution)/shard_map/ppermute | solution.py:29
  719.1 10.8 %collective-permute-done.36 = f32[512,256]{1,0:T(8,128)S(1)} collective-permute-done((f32[512,256]{1,0:T(8,128)S(1)}, f32[512,256]{1,0:T(8,128)S(1)}, u32[]{:S(2)}, u32[]{:S(2)}) %collective-permute-start.36) | collective-permute-done | bytes 524320 | tf_op jit(solution)/shard_map/ppermute | solution.py:29
  739.1 21.6 %collective-permute-done.38 = f32[512,256]{1,0:T(8,128)S(1)} collective-permute-done((f32[512,256]{1,0:T(8,128)S(1)}, f32[512,256]{1,0:T(8,128)S(1)}, u32[]{:S(2)}, u32[]{:S(2)}) %collective-permute-start.38) | collective-permute-done | bytes 524320 | tf_op jit(solution)/shard_map/ppermute | solution.py:49
  760.8 11.2 %collective-permute-done.41 = f32[512,256]{1,0:T(8,128)S(1)} collective-permute-done((f32[512,256]{1,0:T(8,128)S(1)}, f32[512,256]{1,0:T(8,128)S(1)}, u32[]{:S(2)}, u32[]{:S(2)}) %collective-permute-start.41) | collective-permute-done | bytes 524320 | tf_op jit(solution)/shard_map/ppermute | solution.py:49
  772.0 11.2 %collective-permute-done.44 = f32[512,256]{1,0:T(8,128)S(1)} collective-permute-done((f32[512,256]{1,0:T(8,128)S(1)}, f32[512,256]{1,0:T(8,128)S(1)}, u32[]{:S(2)}, u32[]{:S(2)}) %collective-permute-start.44) | collective-permute-done | bytes 524320 | tf_op jit(solution)/shard_map/ppermute | solution.py:49
  783.2 11.2 %collective-permute-done.47 = f32[512,256]{1,0:T(8,128)S(1)} collective-permute-done((f32[512,256]{1,0:T(8,128)S(1)}, f32[512,256]{1,0:T(8,128)S(1)}, u32[]{:S(2)}, u32[]{:S(2)}) %collective-permute-start.47) | collective-permute-done | bytes 524320 | tf_op jit(solution)/shard_map/ppermute | solution.py:49
  796.8 8.1 fusion.26
  805.6 10.2 %multiply_multiply_fusion.1 = f32[4,1024,512]{2,1,0:T(8,128)} fusion(f32[4,1024,512]{2,1,0:T(8,128)} %param.18, f32[4,1024,512]{2,1,0:T(8,128)} %fusion.26, f32[1024,4,256]{2,0,1:T(8,128)S(1)} %bitcast.247, f32[4,256]{1,0:T(4,128)S(1)} %subtract_exponential_fusion.8, f32[4,256]{1,0:T(4,128)S(1)} %fusion.79, f32[1,512,256]{2,1,0:T(8,128)S(1)} %get-tuple-element.60, ...), kind=kOutput, calls=%fused_computation.9 | convolution fusion | flops 3230138368 | bytes 31465472 | tf_op jit(solution)/shard_map/iub,ujb->uij/dot_general | solution.py:174
  815.8 12.5 %fusion.29 = f32[2,4096,512]{2,1,0:T(8,128)} fusion(f32[4096,2,256]{2,0,1:T(8,128)} %all-gather.17.cloned.1.call-done, f32[2,512,512]{2,1,0:T(8,128)S(1)} %copy-done.4), kind=kOutput, calls=%fused_computation.40 | convolution fusion | flops 6442450944 | bytes 26214400 | tf_op jit(solution)/shard_map/igb,gjb->gij/dot_general | solution.py:128
  828.4 19.6 %all-gather.19.cloned.1.call-done = f32[4096,2,256]{2,0,1:T(8,128)} async-done(((f32[512,2,256]{2,0,1:T(8,128)}), f32[4096,2,256]{2,0,1:T(8,128)}) %all-gather.19.cloned.1.call-update) | async-done | bytes 8388624 | tf_op jit(solution)/shard_map/all_gather | solution.py:126
  847.9 22.7 %multiply_multiply_fusion = f32[2,4096,512]{2,1,0:T(8,128)} fusion(f32[2,4096,512]{2,1,0:T(8,128)} %param.17, f32[2,4096,512]{2,1,0:T(8,128)} %fusion.29, f32[4096,2,256]{2,0,1:T(8,128)} %all-gather.19.cloned.1.call-done, f32[2,512,512]{2,1,0:T(8,128)} %copy-done.3), kind=kOutput, calls=%fused_computation | convolution fusion | flops 6455033856 | bytes 59768832 | tf_op jit(solution)/shard_map/igb,gjb->gij/dot_general | solution.py:128
  (272 shorter events, 115.4 us)
Async XLA Ops:
  7.2 191.5 %copy-start = (f32[4,512,256]{2,1,0:T(8,128)S(1)}, f32[4,512,256]{2,1,0:T(8,128)}, u32[]{:S(2)}) copy-start(f32[4,512,256]{2,1,0:T(8,128)} %param.15) | copy-start | bytes 6291460
  7.2 78.2 %reduce-scatter.7.cloned.1.call-start = ((), (), s32[]{:S(2)}) async-start(), calls=%async_computation.6 | async-start | bytes 4718592 | tf_op jit(solution)/shard_map/reduce_scatter | solution.py:92
  33.6 106.9 %reduce-scatter.9.cloned.1.call-start = ((), (), s32[]{:S(2)}) async-start(), calls=%async_computation.7 | async-start | bytes 4718592 | tf_op jit(solution)/shard_map/reduce_scatter | solution.py:92
  42.7 202.0 %reduce-scatter.11.cloned.1.call-start = ((), (), s32[]{:S(2)}) async-start(), calls=%async_computation.8 | async-start | bytes 4718592 | tf_op jit(solution)/shard_map/reduce_scatter | solution.py:92
  52.8 198.5 %reduce-scatter.13.cloned.1.call-start = ((), (), s32[]{:S(2)}) async-start(), calls=%async_computation.9 | async-start | bytes 4718592 | tf_op jit(solution)/shard_map/reduce_scatter | solution.py:92
  61.9 268.8 %reduce-scatter.15.cloned.1.call-start = ((), (), s32[]{:S(2)}) async-start(), calls=%async_computation.10 | async-start | bytes 4718592 | tf_op jit(solution)/shard_map/reduce_scatter | solution.py:148
  142.1 15.7 %collective-permute-start = (f32[512,256]{1,0:T(8,128)S(1)}, f32[512,256]{1,0:T(8,128)S(1)}, u32[]{:S(2)}, u32[]{:S(2)}) collective-permute-start(f32[512,256]{1,0:T(8,128)S(1)} %get-tuple-element.87), channel_id=1, source_target_pairs={{0,8},{24,16},{1,9},{25,17},{2,10},{26,18},{3,11},{27,19},{4,12},{... | collective-permute-start | bytes 1572872 | tf_op jit(solution)/shard_map/ppermute | solution.py:29
  145.5 23.5 %collective-permute-start.9 = (f32[512,256]{1,0:T(8,128)S(1)}, f32[512,256]{1,0:T(8,128)S(1)}, u32[]{:S(2)}, u32[]{:S(2)}) collective-permute-start(f32[512,256]{1,0:T(8,128)S(1)} %get-tuple-element.90), channel_id=1, source_target_pairs={{0,8},{24,16},{1,9},{25,17},{2,10},{26,18},{3,11},{27,19},{4,12},{... | collective-permute-start | bytes 1572872 | tf_op jit(solution)/shard_map/ppermute | solution.py:29
  146.8 33.4 %collective-permute-start.6 = (f32[512,256]{1,0:T(8,128)S(1)}, f32[512,256]{1,0:T(8,128)S(1)}, u32[]{:S(2)}, u32[]{:S(2)}) collective-permute-start(f32[512,256]{1,0:T(8,128)S(1)} %get-tuple-element.89), channel_id=1, source_target_pairs={{0,8},{24,16},{1,9},{25,17},{2,10},{26,18},{3,11},{27,19},{4,12},{... | collective-permute-start | bytes 1572872 | tf_op jit(solution)/shard_map/ppermute | solution.py:29
  148.2 42.2 %collective-permute-start.3 = (f32[512,256]{1,0:T(8,128)S(1)}, f32[512,256]{1,0:T(8,128)S(1)}, u32[]{:S(2)}, u32[]{:S(2)}) collective-permute-start(f32[512,256]{1,0:T(8,128)S(1)} %get-tuple-element.88), channel_id=1, source_target_pairs={{0,8},{24,16},{1,9},{25,17},{2,10},{26,18},{3,11},{27,19},{4,12},{... | collective-permute-start | bytes 1572872 | tf_op jit(solution)/shard_map/ppermute | solution.py:29
  157.8 33.3 %collective-permute-start.1 = (f32[512,256]{1,0:T(8,128)S(1)}, f32[512,256]{1,0:T(8,128)S(1)}, u32[]{:S(2)}, u32[]{:S(2)}) collective-permute-start(f32[512,256]{1,0:T(8,128)S(1)} %add.292), channel_id=1, source_target_pairs={{8,16},{16,8},{9,17},{17,9},{10,18},{18,10},{11,19},{19,11},{12,20... | collective-permute-start | bytes 1572872 | tf_op jit(solution)/shard_map/ppermute | solution.py:39
  169.1 23.6 %collective-permute-start.10 = (f32[512,256]{1,0:T(8,128)S(1)}, f32[512,256]{1,0:T(8,128)S(1)}, u32[]{:S(2)}, u32[]{:S(2)}) collective-permute-start(f32[512,256]{1,0:T(8,128)S(1)} %add.304), channel_id=1, source_target_pairs={{8,16},{16,8},{9,17},{17,9},{10,18},{18,10},{11,19},{19,11},{12,20... | collective-permute-start | bytes 1572872 | tf_op jit(solution)/shard_map/ppermute | solution.py:39
  180.3 13.7 %collective-permute-start.7 = (f32[512,256]{1,0:T(8,128)S(1)}, f32[512,256]{1,0:T(8,128)S(1)}, u32[]{:S(2)}, u32[]{:S(2)}) collective-permute-start(f32[512,256]{1,0:T(8,128)S(1)} %add.300), channel_id=1, source_target_pairs={{8,16},{16,8},{9,17},{17,9},{10,18},{18,10},{11,19},{19,11},{12,20... | collective-permute-start | bytes 1572872 | tf_op jit(solution)/shard_map/ppermute | solution.py:39
  190.4 5.8 collective-permute-start.4
  191.2 19.5 %collective-permute-start.2 = (f32[512,256]{1,0:T(8,128)S(1)}, f32[512,256]{1,0:T(8,128)}, u32[]{:S(2)}, u32[]{:S(2)}) collective-permute-start(f32[512,256]{1,0:T(8,128)S(1)} %add.293), channel_id=1, source_target_pairs={{8,0},{16,24},{9,1},{17,25},{10,2},{18,26},{11,3},{19,27},{12,4},{... | collective-permute-start | bytes 1572872 | tf_op jit(solution)/shard_map/ppermute | solution.py:49
  192.8 29.2 %collective-permute-start.11 = (f32[512,256]{1,0:T(8,128)S(1)}, f32[512,256]{1,0:T(8,128)}, u32[]{:S(2)}, u32[]{:S(2)}) collective-permute-start(f32[512,256]{1,0:T(8,128)S(1)} %add.305), channel_id=1, source_target_pairs={{8,0},{16,24},{9,1},{17,25},{10,2},{18,26},{11,3},{19,27},{12,4},{... | collective-permute-start | bytes 1572872 | tf_op jit(solution)/shard_map/ppermute | solution.py:49
  194.9 38.3 %collective-permute-start.8 = (f32[512,256]{1,0:T(8,128)}, f32[512,256]{1,0:T(8,128)}, u32[]{:S(2)}, u32[]{:S(2)}) collective-permute-start(f32[512,256]{1,0:T(8,128)} %add.301), channel_id=1, source_target_pairs={{8,0},{16,24},{9,1},{17,25},{10,2},{18,26},{11,3},{19,27},{12,4},{... | collective-permute-start | bytes 1572872 | tf_op jit(solution)/shard_map/ppermute | solution.py:49
  197.1 45.3 %collective-permute-start.5 = (f32[512,256]{1,0:T(8,128)}, f32[512,256]{1,0:T(8,128)}, u32[]{:S(2)}, u32[]{:S(2)}) collective-permute-start(f32[512,256]{1,0:T(8,128)} %add.297), channel_id=1, source_target_pairs={{8,0},{16,24},{9,1},{17,25},{10,2},{18,26},{11,3},{19,27},{12,4},{... | collective-permute-start | bytes 1572872 | tf_op jit(solution)/shard_map/ppermute | solution.py:49
  200.7 43.9 %copy-start.5 = (f32[4,512,512]{2,1,0:T(8,128)}, f32[4,512,512]{2,1,0:T(8,128)S(1)}, u32[]{:S(2)}) copy-start(f32[4,512,512]{2,1,0:T(8,128)S(1)} %convolution_bitcast_fusion.2) | copy-start | bytes 12582916
  244.6 194.9 %copy-start.11 = (f32[1,512,256]{2,1,0:T(8,128)}, f32[1,512,256]{2,1,0:T(8,128)S(1)}, u32[]{:S(2)}) copy-start(f32[1,512,256]{2,1,0:T(8,128)S(1)} %get-tuple-element.63) | copy-start | bytes 1572868
  244.6 194.9 %copy-start.13 = (f32[1,512,256]{2,1,0:T(8,128)}, f32[1,512,256]{2,1,0:T(8,128)S(1)}, u32[]{:S(2)}) copy-start(f32[1,512,256]{2,1,0:T(8,128)S(1)} %get-tuple-element.64) | copy-start | bytes 1572868
  253.8 22.7 %collective-permute-start.12 = (f32[512,256]{1,0:T(8,128)}, f32[512,256]{1,0:T(8,128)}, u32[]{:S(2)}, u32[]{:S(2)}) collective-permute-start(f32[512,256]{1,0:T(8,128)} %get-tuple-element.86), channel_id=1, source_target_pairs={{0,8},{24,16},{1,9},{25,17},{2,10},{26,18},{3,11},{27,19},{4,12},{... | collective-permute-start | bytes 1572872 | tf_op jit(solution)/shard_map/ppermute | solution.py:29
  280.2 148.4 %all-gather.21.cloned.1.call-start = ((), (), s32[]{:S(2)}) async-start(), calls=%async_computation.14 | async-start | bytes 4718592 | tf_op jit(solution)/shard_map/all_gather | solution.py:160
  281.2 13.5 %collective-permute-start.14 = (f32[512,256]{1,0:T(8,128)S(1)}, f32[512,256]{1,0:T(8,128)S(1)}, u32[]{:S(2)}, u32[]{:S(2)}) collective-permute-start(f32[512,256]{1,0:T(8,128)S(1)} %copy-done.41), channel_id=1, source_target_pairs={{0,8},{24,16},{1,9},{25,17},{2,10},{26,18},{3,11},{27,19},{4,12},{... | collective-permute-start | bytes 1572872 | tf_op jit(solution)/shard_map/ppermute | solution.py:29
  282.6 23.4 %collective-permute-start.16 = (f32[512,256]{1,0:T(8,128)S(1)}, f32[512,256]{1,0:T(8,128)S(1)}, u32[]{:S(2)}, u32[]{:S(2)}) collective-permute-start(f32[512,256]{1,0:T(8,128)S(1)} %get-tuple-element.85), channel_id=1, source_target_pairs={{0,8},{24,16},{1,9},{25,17},{2,10},{26,18},{3,11},{27,19},{4,12},{... | collective-permute-start | bytes 1572872 | tf_op jit(solution)/shard_map/ppermute | solution.py:29
  283.9 33.0 %collective-permute-start.18 = (f32[512,256]{1,0:T(8,128)S(1)}, f32[512,256]{1,0:T(8,128)S(1)}, u32[]{:S(2)}, u32[]{:S(2)}) collective-permute-start(f32[512,256]{1,0:T(8,128)S(1)} %get-tuple-element.83), channel_id=1, source_target_pairs={{0,8},{24,16},{1,9},{25,17},{2,10},{26,18},{3,11},{27,19},{4,12},{... | collective-permute-start | bytes 1572872 | tf_op jit(solution)/shard_map/ppermute | solution.py:29
  285.2 35.3 %collective-permute-start.13 = (f32[512,256]{1,0:T(8,128)S(1)}, f32[512,256]{1,0:T(8,128)}, u32[]{:S(2)}, u32[]{:S(2)}) collective-permute-start(f32[512,256]{1,0:T(8,128)S(1)} %add.314), channel_id=1, source_target_pairs={{8,16},{16,8},{9,17},{17,9},{10,18},{18,10},{11,19},{19,11},{12,20... | collective-permute-start | bytes 1572872 | tf_op jit(solution)/shard_map/ppermute | solution.py:39
  295.8 26.6 %collective-permute-start.15 = (f32[512,256]{1,0:T(8,128)S(1)}, f32[512,256]{1,0:T(8,128)}, u32[]{:S(2)}, u32[]{:S(2)}) collective-permute-start(f32[512,256]{1,0:T(8,128)S(1)} %add.317), channel_id=1, source_target_pairs={{8,16},{16,8},{9,17},{17,9},{10,18},{18,10},{11,19},{19,11},{12,20... | collective-permute-start | bytes 1572872 | tf_op jit(solution)/shard_map/ppermute | solution.py:39
  307.1 17.3 %collective-permute-start.17 = (f32[512,256]{1,0:T(8,128)S(1)}, f32[512,256]{1,0:T(8,128)}, u32[]{:S(2)}, u32[]{:S(2)}) collective-permute-start(f32[512,256]{1,0:T(8,128)S(1)} %add.320), channel_id=1, source_target_pairs={{8,16},{16,8},{9,17},{17,9},{10,18},{18,10},{11,19},{19,11},{12,20... | collective-permute-start | bytes 1572872 | tf_op jit(solution)/shard_map/ppermute | solution.py:39
  317.0 9.3 %collective-permute-start.19 = (f32[512,256]{1,0:T(8,128)S(1)}, f32[512,256]{1,0:T(8,128)}, u32[]{:S(2)}, u32[]{:S(2)}) collective-permute-start(f32[512,256]{1,0:T(8,128)S(1)} %add.323), channel_id=1, source_target_pairs={{8,16},{16,8},{9,17},{17,9},{10,18},{18,10},{11,19},{19,11},{12,20... | collective-permute-start | bytes 1572872 | tf_op jit(solution)/shard_map/ppermute | solution.py:39
  337.3 217.6 %reduce-scatter.17.cloned.1.call-start = ((), (), s32[]{:S(2)}) async-start(), calls=%async_computation.11 | async-start | bytes 4718592 | tf_op jit(solution)/shard_map/reduce_scatter | solution.py:148
  337.4 83.5 %collective-permute-start.20 = (f32[512,256]{1,0:T(8,128)S(1)}, f32[512,256]{1,0:T(8,128)}, u32[]{:S(2)}, u32[]{:S(2)}) collective-permute-start(f32[512,256]{1,0:T(8,128)S(1)} %copy-done.28), channel_id=1, source_target_pairs={{8,0},{16,24},{9,1},{17,25},{10,2},{18,26},{11,3},{19,27},{12,4},{... | collective-permute-start | bytes 1572872 | tf_op jit(solution)/shard_map/ppermute | solution.py:49
  338.7 84.1 %collective-permute-start.21 = (f32[512,256]{1,0:T(8,128)S(1)}, f32[512,256]{1,0:T(8,128)}, u32[]{:S(2)}, u32[]{:S(2)}) collective-permute-start(f32[512,256]{1,0:T(8,128)S(1)} %copy-done.29), channel_id=1, source_target_pairs={{8,0},{16,24},{9,1},{17,25},{10,2},{18,26},{11,3},{19,27},{12,4},{... | collective-permute-start | bytes 1572872 | tf_op jit(solution)/shard_map/ppermute | solution.py:49
  340.0 84.7 %collective-permute-start.22 = (f32[512,256]{1,0:T(8,128)S(1)}, f32[512,256]{1,0:T(8,128)}, u32[]{:S(2)}, u32[]{:S(2)}) collective-permute-start(f32[512,256]{1,0:T(8,128)S(1)} %copy-done.30), channel_id=1, source_target_pairs={{8,0},{16,24},{9,1},{17,25},{10,2},{18,26},{11,3},{19,27},{12,4},{... | collective-permute-start | bytes 1572872 | tf_op jit(solution)/shard_map/ppermute | solution.py:49
  341.3 85.4 %collective-permute-start.23 = (f32[512,256]{1,0:T(8,128)S(1)}, f32[512,256]{1,0:T(8,128)}, u32[]{:S(2)}, u32[]{:S(2)}) collective-permute-start(f32[512,256]{1,0:T(8,128)S(1)} %copy-done.31), channel_id=1, source_target_pairs={{8,0},{16,24},{9,1},{17,25},{10,2},{18,26},{11,3},{19,27},{12,4},{... | collective-permute-start | bytes 1572872 | tf_op jit(solution)/shard_map/ppermute | solution.py:49
  452.5 27.7 %collective-permute-start.30 = (f32[512,256]{1,0:T(8,128)}, f32[512,256]{1,0:T(8,128)}, u32[]{:S(2)}, u32[]{:S(2)}) collective-permute-start(f32[512,256]{1,0:T(8,128)} %get-tuple-element.79), channel_id=1, source_target_pairs={{0,8},{24,16},{1,9},{25,17},{2,10},{26,18},{3,11},{27,19},{4,12},{... | collective-permute-start | bytes 1572872 | tf_op jit(solution)/shard_map/ppermute | solution.py:29
  454.7 25.5 %collective-permute-start.28 = (f32[512,256]{1,0:T(8,128)}, f32[512,256]{1,0:T(8,128)}, u32[]{:S(2)}, u32[]{:S(2)}) collective-permute-start(f32[512,256]{1,0:T(8,128)} %get-tuple-element.80), channel_id=1, source_target_pairs={{0,8},{24,16},{1,9},{25,17},{2,10},{26,18},{3,11},{27,19},{4,12},{... | collective-permute-start | bytes 1572872 | tf_op jit(solution)/shard_map/ppermute | solution.py:29
  456.8 32.1 %collective-permute-start.26 = (f32[512,256]{1,0:T(8,128)}, f32[512,256]{1,0:T(8,128)}, u32[]{:S(2)}, u32[]{:S(2)}) collective-permute-start(f32[512,256]{1,0:T(8,128)} %get-tuple-element.81), channel_id=1, source_target_pairs={{0,8},{24,16},{1,9},{25,17},{2,10},{26,18},{3,11},{27,19},{4,12},{... | collective-permute-start | bytes 1572872 | tf_op jit(solution)/shard_map/ppermute | solution.py:29
  459.0 40.9 %collective-permute-start.24 = (f32[512,256]{1,0:T(8,128)}, f32[512,256]{1,0:T(8,128)}, u32[]{:S(2)}, u32[]{:S(2)}) collective-permute-start(f32[512,256]{1,0:T(8,128)} %get-tuple-element.82), channel_id=1, source_target_pairs={{0,8},{24,16},{1,9},{25,17},{2,10},{26,18},{3,11},{27,19},{4,12},{... | collective-permute-start | bytes 1572872 | tf_op jit(solution)/shard_map/ppermute | solution.py:29
  505.2 109.1 %all-gather.23.cloned.1.call-start = ((), (), s32[]{:S(2)}) async-start(), calls=%async_computation.15 | async-start | bytes 4718592 | tf_op jit(solution)/shard_map/all_gather | solution.py:160
  506.2 3.1 collective-permute-start.25
  507.0 3.4 collective-permute-start.27
  507.7 3.8 collective-permute-start.29
  508.5 3.2 collective-permute-start.31
  562.1 253.7 %all-gather.17.cloned.1.call-start = ((), (), s32[]{:S(2)}) async-start(), calls=%async_computation.12 | async-start | bytes 9437184 | tf_op jit(solution)/shard_map/all_gather | solution.py:126
  562.1 17.4 %collective-permute-start.32 = (f32[512,256]{1,0:T(8,128)S(1)}, f32[512,256]{1,0:T(8,128)S(1)}, u32[]{:S(2)}, u32[]{:S(2)}) collective-permute-start(f32[512,256]{1,0:T(8,128)S(1)} %add.335), channel_id=1, source_target_pairs={{8,0},{16,24},{9,1},{17,25},{10,2},{18,26},{11,3},{19,27},{12,4},{... | collective-permute-start | bytes 1572872 | tf_op jit(solution)/shard_map/ppermute | solution.py:49
  563.4 27.3 %collective-permute-start.33 = (f32[512,256]{1,0:T(8,128)S(1)}, f32[512,256]{1,0:T(8,128)S(1)}, u32[]{:S(2)}, u32[]{:S(2)}) collective-permute-start(f32[512,256]{1,0:T(8,128)S(1)} %add.337), channel_id=1, source_target_pairs={{8,0},{16,24},{9,1},{17,25},{10,2},{18,26},{11,3},{19,27},{12,4},{... | collective-permute-start | bytes 1572872 | tf_op jit(solution)/shard_map/ppermute | solution.py:49
  564.7 37.2 %collective-permute-start.34 = (f32[512,256]{1,0:T(8,128)S(1)}, f32[512,256]{1,0:T(8,128)S(1)}, u32[]{:S(2)}, u32[]{:S(2)}) collective-permute-start(f32[512,256]{1,0:T(8,128)S(1)} %add.339), channel_id=1, source_target_pairs={{8,0},{16,24},{9,1},{17,25},{10,2},{18,26},{11,3},{19,27},{12,4},{... | collective-permute-start | bytes 1572872 | tf_op jit(solution)/shard_map/ppermute | solution.py:49
  566.0 45.4 %collective-permute-start.35 = (f32[512,256]{1,0:T(8,128)S(1)}, f32[512,256]{1,0:T(8,128)S(1)}, u32[]{:S(2)}, u32[]{:S(2)}) collective-permute-start(f32[512,256]{1,0:T(8,128)S(1)} %add.341), channel_id=1, source_target_pairs={{8,0},{16,24},{9,1},{17,25},{10,2},{18,26},{11,3},{19,27},{12,4},{... | collective-permute-start | bytes 1572872 | tf_op jit(solution)/shard_map/ppermute | solution.py:49
  619.6 228.4 %all-gather.19.cloned.1.call-start = ((), (), s32[]{:S(2)}) async-start(), calls=%async_computation.13 | async-start | bytes 9437184 | tf_op jit(solution)/shard_map/all_gather | solution.py:126
  683.1 13.5 %collective-permute-start.45 = (f32[512,256]{1,0:T(8,128)S(1)}, f32[512,256]{1,0:T(8,128)S(1)}, u32[]{:S(2)}, u32[]{:S(2)}) collective-permute-start(f32[512,256]{1,0:T(8,128)S(1)} %get-tuple-element.71), channel_id=1, source_target_pairs={{0,8},{24,16},{1,9},{25,17},{2,10},{26,18},{3,11},{27,19},{4,12},{... | collective-permute-start | bytes 1572872 | tf_op jit(solution)/shard_map/ppermute | solution.py:29
  684.5 23.4 %collective-permute-start.42 = (f32[512,256]{1,0:T(8,128)S(1)}, f32[512,256]{1,0:T(8,128)S(1)}, u32[]{:S(2)}, u32[]{:S(2)}) collective-permute-start(f32[512,256]{1,0:T(8,128)S(1)} %get-tuple-element.72), channel_id=1, source_target_pairs={{0,8},{24,16},{1,9},{25,17},{2,10},{26,18},{3,11},{27,19},{4,12},{... | collective-permute-start | bytes 1572872 | tf_op jit(solution)/shard_map/ppermute | solution.py:29
  685.8 33.3 %collective-permute-start.39 = (f32[512,256]{1,0:T(8,128)S(1)}, f32[512,256]{1,0:T(8,128)S(1)}, u32[]{:S(2)}, u32[]{:S(2)}) collective-permute-start(f32[512,256]{1,0:T(8,128)S(1)} %get-tuple-element.73), channel_id=1, source_target_pairs={{0,8},{24,16},{1,9},{25,17},{2,10},{26,18},{3,11},{27,19},{4,12},{... | collective-permute-start | bytes 1572872 | tf_op jit(solution)/shard_map/ppermute | solution.py:29
  687.1 42.8 %collective-permute-start.36 = (f32[512,256]{1,0:T(8,128)S(1)}, f32[512,256]{1,0:T(8,128)S(1)}, u32[]{:S(2)}, u32[]{:S(2)}) collective-permute-start(f32[512,256]{1,0:T(8,128)S(1)} %get-tuple-element.74), channel_id=1, source_target_pairs={{0,8},{24,16},{1,9},{25,17},{2,10},{26,18},{3,11},{27,19},{4,12},{... | collective-permute-start | bytes 1572872 | tf_op jit(solution)/shard_map/ppermute | solution.py:29
  730.4 2.8 collective-permute-start.37
  731.1 3.6 collective-permute-start.40
  731.8 4.3 collective-permute-start.43
  732.5 5.0 collective-permute-start.46
  733.3 61.1 %copy-start.36 = (f32[512,256]{1,0:T(8,128)S(1)}, f32[512,256]{1,0:T(8,128)}, u32[]{:S(2)}) copy-start(f32[512,256]{1,0:T(8,128)} %reduce-scatter.11.cloned.1.call-done) | copy-start | bytes 1572868
  733.3 61.1 %copy-start.37 = (f32[512,256]{1,0:T(8,128)S(1)}, f32[512,256]{1,0:T(8,128)}, u32[]{:S(2)}) copy-start(f32[512,256]{1,0:T(8,128)} %reduce-scatter.13.cloned.1.call-done) | copy-start | bytes 1572868
  733.3 27.5 %collective-permute-start.38 = (f32[512,256]{1,0:T(8,128)S(1)}, f32[512,256]{1,0:T(8,128)S(1)}, u32[]{:S(2)}, u32[]{:S(2)}) collective-permute-start(f32[512,256]{1,0:T(8,128)S(1)} %add.353), channel_id=1, source_target_pairs={{8,0},{16,24},{9,1},{17,25},{10,2},{18,26},{11,3},{19,27},{12,4},{... | collective-permute-start | bytes 1572872 | tf_op jit(solution)/shard_map/ppermute | solution.py:49
  734.8 37.2 %collective-permute-start.41 = (f32[512,256]{1,0:T(8,128)S(1)}, f32[512,256]{1,0:T(8,128)S(1)}, u32[]{:S(2)}, u32[]{:S(2)}) collective-permute-start(f32[512,256]{1,0:T(8,128)S(1)} %add.355), channel_id=1, source_target_pairs={{8,0},{16,24},{9,1},{17,25},{10,2},{18,26},{11,3},{19,27},{12,4},{... | collective-permute-start | bytes 1572872 | tf_op jit(solution)/shard_map/ppermute | solution.py:49
  736.2 47.0 %collective-permute-start.44 = (f32[512,256]{1,0:T(8,128)S(1)}, f32[512,256]{1,0:T(8,128)S(1)}, u32[]{:S(2)}, u32[]{:S(2)}) collective-permute-start(f32[512,256]{1,0:T(8,128)S(1)} %add.358), channel_id=1, source_target_pairs={{8,0},{16,24},{9,1},{17,25},{10,2},{18,26},{11,3},{19,27},{12,4},{... | collective-permute-start | bytes 1572872 | tf_op jit(solution)/shard_map/ppermute | solution.py:49
  737.6 56.8 %collective-permute-start.47 = (f32[512,256]{1,0:T(8,128)S(1)}, f32[512,256]{1,0:T(8,128)S(1)}, u32[]{:S(2)}, u32[]{:S(2)}) collective-permute-start(f32[512,256]{1,0:T(8,128)S(1)} %add.361), channel_id=1, source_target_pairs={{8,0},{16,24},{9,1},{17,25},{10,2},{18,26},{11,3},{19,27},{12,4},{... | collective-permute-start | bytes 1572872 | tf_op jit(solution)/shard_map/ppermute | solution.py:49
  (46 other events, 487.3 us)
Sparse Core Ops, SparseCore 0:
  33.7 51.6 reduce-scatter.6
  89.1 51.3 reduce-scatter.8
  144.4 51.2 reduce-scatter.10
  199.9 51.3 reduce-scatter.12
  280.3 50.3 reduce-scatter.14
  337.5 42.7 all-gather.20
  505.3 49.5 reduce-scatter.16
  562.2 37.3 all-gather.22
  619.7 54.5 all-gather.16
  796.2 51.6 all-gather.18

commit v2 on v1

--- a/solution.py
+++ b/solution.py
@@ -3,7 +3,7 @@
 from jax import lax
 from jax.sharding import PartitionSpec as P
 
-CHUNKS = 2
+CHUNKS = 1
 
 
 def one_hot(pixels, values):

time: 887 us -> 931 us (1.050)
  waiting for transfers between devices: 410 us -> 652 us
  blocking collectives: 144 us -> 61.2 us
  matrix products: 140 us -> 102 us
  starting transfers between devices: 66 us -> 32 us
  other arithmetic: 63.4 us -> 31.6 us
  local copies, waits for them, and re-layouts: 32.8 us -> 22.4 us
    all_gather x2 -> x1, blocking collectives: 118 us -> 41.6 us  [shards(): lax.all_gather(jnp.stack([root_local, jnp.sum(expo_root, axis=0)]), ('lea...]
    all_gather x2 -> x1, waiting for transfers between devices: 19.6 us -> 75.5 us  [collect(): t_grand = lax.all_gather(ratio_own, 'panel', axis=0, tiled=True)]
    ppermute x16 -> x8, waiting for transfers between devices: 141 us -> 196 us  [outward(): received = lax.ppermute(total, axis, pairs)]
    reduce_scatter x4 -> x2, waiting for transfers between devices: 78.8 us -> 129 us  [shards(): lax.psum_scatter(jnp.dot(weight_grand[g], e_grand[g, :, here], precision=...]
    ppermute x16 -> x8, waiting for transfers between devices: 125 us -> 168 us  [inward(): return total + lax.ppermute(total, axis, pairs)]
    reduce_scatter x2 -> x1, waiting for transfers between devices: 45.7 us -> 68.8 us  [shards(): lax.psum_scatter(partial * shift[None], 'panel', scatter_dimension=0, til...]
    all_gather x2 -> x1, waiting for transfers between devices: 0.01 us -> 14.5 us  [shards(): t_rows = lax.all_gather(expo_root[:, None, :] / s_mid, 'panel', axis=0)]
    ppermute x16 -> x8, starting transfers between devices: 29.4 us -> 15.1 us  [inward(): return total + lax.ppermute(total, axis, pairs)]
  transfers between devices with their start and end apart: 58 -> 29, of which waited for: 31 -> 21; matrix products, arithmetic and copies ran while one was open for 16% -> 4% of each run, Pallas kernels for 0% -> 0%
where the time goes in v2:
time: 931 us; the launch traced here: 921 us
  waiting for transfers between devices  652 us (70%)
  matrix products  102 us (11%)
  blocking collectives  61.2 us (7%)
  starting transfers between devices  32 us (3%)
  other arithmetic  31.6 us (3%)
  local copies, waits for them, and re-layouts  22.4 us (2%)
  between operations  19.8 us (2%)
    ppermute x8, waiting for transfers between devices, outward(): received = lax.ppermute(total, axis, pairs)  196 us
    ppermute x8, waiting for transfers between devices, inward(): return total + lax.ppermute(total, axis, pairs)  168 us
    reduce_scatter x2, waiting for transfers between devices, shards(): lax.psum_scatter(jnp.dot(weight_grand[g], e_grand[g, :, here], precision=...  129 us
    all_gather x1, waiting for transfers between devices, collect(): t_grand = lax.all_gather(ratio_own, 'panel', axis=0, tiled=True)  75.5 us
    reduce_scatter x1, waiting for transfers between devices, shards(): lax.psum_scatter(partial * shift[None], 'panel', scatter_dimension=0, til...  68.8 us
    all_gather x1, blocking collectives, shards(): lax.all_gather(jnp.stack([root_local, jnp.sum(expo_root, axis=0)]), ('lea...  41.6 us
    dot_general x1, matrix products, collect(): jnp.einsum('igb,gjb->gij', t_grand, e_grand[:, :, here], precision=high)  23.5 us
    dot_general x2, matrix products, shards(): jnp.dot(weight_grand[g], e_grand[g, :, here], precision=high)  22.8 us
  transfers between devices with their start and end apart: 29, of which 21 were waited for; matrix products, arithmetic and copies ran while one was open for 4% of the time, Pallas kernels for 0%

profile of v2, /device:TPU:0, one launch (start us, length us, event | category | flops | bytes accessed | tf_op | source)
XLA Modules:
  0.0 921.4 jit_solution(3187846633618657357)
XLA Ops:
  7.2 3.8 bitcast_reduce_fusion
  11.0 10.5 %all-gather.4 = f32[8,2,512]{2,1,0:T(2,128)S(1)} all-gather(f32[1,2,512]{2,1,0:T(2,128)S(1)} %bitcast.140), channel_id=2, replica_groups=mesh['leaf'=4,'panel'=8] {'panel'}, dimensions={0}, use_global_device_ids=true | all-gather | bytes 36864 | tf_op jit(solution)/shard_map/all_gather | solution.py:80
  21.5 1.9 fusion.16
  23.4 1.3 copy-done.3
  24.7 11.1 %fusion.9 = f32[4096,512]{1,0:T(8,128)} fusion(f32[2,4096,512]{2,1,0:T(8,128)} %param.17, f32[2,512,512]{2,1,0:T(8,128)S(1)} %fusion.16), kind=kOutput, calls=%fused_computation.9 | convolution fusion | flops 6442450944 | bytes 17825792 | tf_op jit(solution)/shard_map/dot_general | solution.py:93
  35.9 11.7 %fusion.6 = f32[4096,512]{1,0:T(8,128)} fusion(f32[2,4096,512]{2,1,0:T(8,128)} %param.17, f32[2,512,512]{2,1,0:T(8,128)} %copy-done.3), kind=kOutput, calls=%fused_computation.8 | convolution fusion | flops 6442450944 | bytes 17825792 | tf_op jit(solution)/shard_map/dot_general | solution.py:93
  54.1 53.6 %reduce-scatter.6.cloned.1.call-done = f32[512,512]{1,0:T(8,128)} async-done(((f32[4096,512]{1,0:T(8,128)}), f32[512,512]{1,0:T(8,128)}) %reduce-scatter.6.cloned.1.call-update) | async-done | bytes 1048592 | tf_op jit(solution)/shard_map/reduce_scatter | solution.py:92
  107.6 75.8 %reduce-scatter.4.cloned.1.call-done = f32[512,512]{1,0:T(8,128)} async-done(((f32[4096,512]{1,0:T(8,128)}), f32[512,512]{1,0:T(8,128)}) %reduce-scatter.4.cloned.1.call-update) | async-done | bytes 1048592 | tf_op jit(solution)/shard_map/reduce_scatter | solution.py:92
  183.4 2.3 select_add_fusion.3
  185.7 3.4 collective-permute-start
  189.1 1.4 collective-permute-start.3
  190.5 1.4 collective-permute-start.6
  191.8 1.4 collective-permute-start.9
  193.2 19.4 %collective-permute-done = f32[512,512]{1,0:T(8,128)S(1)} collective-permute-done((f32[512,512]{1,0:T(8,128)S(1)}, f32[512,512]{1,0:T(8,128)S(1)}, u32[]{:S(2)}, u32[]{:S(2)}) %collective-permute-start) | collective-permute-done | bytes 1048608 | tf_op jit(solution)/shard_map/ppermute | solution.py:29
  213.5 21.5 %collective-permute-done.3 = f32[512,512]{1,0:T(8,128)S(1)} collective-permute-done((f32[512,512]{1,0:T(8,128)S(1)}, f32[512,512]{1,0:T(8,128)S(1)}, u32[]{:S(2)}, u32[]{:S(2)}) %collective-permute-start.3) | collective-permute-done | bytes 1048608 | tf_op jit(solution)/shard_map/ppermute | solution.py:29
  236.0 21.5 %collective-permute-done.6 = f32[512,512]{1,0:T(8,128)S(1)} collective-permute-done((f32[512,512]{1,0:T(8,128)S(1)}, f32[512,512]{1,0:T(8,128)S(1)}, u32[]{:S(2)}, u32[]{:S(2)}) %collective-permute-start.6) | collective-permute-done | bytes 1048608 | tf_op jit(solution)/shard_map/ppermute | solution.py:29
  258.8 20.0 %collective-permute-done.9 = f32[512,512]{1,0:T(8,128)S(1)} collective-permute-done((f32[512,512]{1,0:T(8,128)S(1)}, f32[512,512]{1,0:T(8,128)S(1)}, u32[]{:S(2)}, u32[]{:S(2)}) %collective-permute-start.9) | collective-permute-done | bytes 1048608 | tf_op jit(solution)/shard_map/ppermute | solution.py:29
  280.1 1.4 collective-permute-start.2
  281.5 1.2 add.160
  282.7 1.3 collective-permute-start.5
  284.0 1.2 add.164
  285.3 1.3 collective-permute-start.8
  286.6 1.2 add.168
  287.7 1.3 collective-permute-start.11
  289.1 2.1 convolution_bitcast_fusion.1
  291.1 19.7 %collective-permute-done.2 = f32[512,512]{1,0:T(8,128)} collective-permute-done((f32[512,512]{1,0:T(8,128)S(1)}, f32[512,512]{1,0:T(8,128)}, u32[]{:S(2)}, u32[]{:S(2)}) %collective-permute-start.2) | collective-permute-done | bytes 1048608 | tf_op jit(solution)/shard_map/ppermute | solution.py:49
  310.8 22.5 %collective-permute-done.5 = f32[512,512]{1,0:T(8,128)} collective-permute-done((f32[512,512]{1,0:T(8,128)}, f32[512,512]{1,0:T(8,128)}, u32[]{:S(2)}, u32[]{:S(2)}) %collective-permute-start.5) | collective-permute-done | bytes 1048608 | tf_op jit(solution)/shard_map/ppermute | solution.py:49
  333.3 22.5 %collective-permute-done.8 = f32[512,512]{1,0:T(8,128)} collective-permute-done((f32[512,512]{1,0:T(8,128)}, f32[512,512]{1,0:T(8,128)}, u32[]{:S(2)}, u32[]{:S(2)}) %collective-permute-start.8) | collective-permute-done | bytes 1048608 | tf_op jit(solution)/shard_map/ppermute | solution.py:49
  355.7 20.4 %collective-permute-done.11 = f32[512,512]{1,0:T(8,128)} collective-permute-done((f32[512,512]{1,0:T(8,128)}, f32[512,512]{1,0:T(8,128)}, u32[]{:S(2)}, u32[]{:S(2)}) %collective-permute-start.11) | collective-permute-done | bytes 1048608 | tf_op jit(solution)/shard_map/ppermute | solution.py:49
  376.1 3.7 fusion.28
  381.3 9.1 all-gather.5
  390.4 16.8 %convolution_bitcast_fusion = f32[1024,4,512]{0,2,1:T(8,128)S(1)} fusion(f32[4,1024,512]{2,1,0:T(8,128)} %param.18, f32[4,512]{1,0:T(4,128)S(1)} %fusion.44, f32[1,512,512]{2,1,0:T(8,128)S(1)} %get-tuple-element.16, f32[1,512,512]{2,1,0:T(8,128)S(1)} %get-tuple-element.17, f32[1,512,512]{2,1,0:T(8,128)} %copy-done.2, f32[1,512,512]{2,1,0:T(8,128)S(1)} %get-tuple-element.15), kind=kOutput, calls=%fused_computation.17 | convolution fusion | flops 6446645248 | bytes 20979712 | tf_op jit(solution)/shard_map/uij,ujb->iub/dot_general | solution.py:135
  407.2 4.0 broadcast_multiply_fusion.1
  412.0 68.8 %reduce-scatter.8.cloned.1.call-done = f32[128,4,512]{0,2,1:T(8,128)} async-done(((f32[1024,4,512]{0,2,1:T(8,128)}), f32[128,4,512]{0,2,1:T(8,128)}) %reduce-scatter.8.cloned.1.call-update) | async-done | bytes 1048592 | tf_op jit(solution)/shard_map/reduce_scatter | solution.py:148
  480.8 2.3 add_reduce_fusion
  484.2 1.3 fusion.49
  487.3 2.3 broadcast_divide_fusion
  489.8 41.6 %all-gather.6 = f32[32,2,512]{2,1,0:T(2,128)S(1)} all-gather(f32[1,2,512]{2,1,0:T(2,128)S(1)} %maximum_bitcast_fusion), channel_id=4, replica_groups=mesh['leaf'=4,'panel'=8] {'leaf','panel'}, dimensions={0}, use_global_device_ids=true | all-gather | bytes 135168 | tf_op jit(solution)/shard_map/all_gather | solution.py:157
  531.7 14.5 %all-gather.12.cloned.1.call-done = f32[1024,4,512]{0,2,1:T(8,128)} async-done(((f32[128,4,512]{0,2,1:T(8,128)}), f32[1024,4,512]{0,2,1:T(8,128)}) %all-gather.12.cloned.1.call-update) | async-done | bytes 8388624 | tf_op jit(solution)/shard_map/all_gather | solution.py:160
  546.2 5.5 copy.56
  551.7 3.8 broadcast_multiply_fusion
  555.5 9.9 %copy.45 = f32[8,128,4,512]{3,1,0,2:T(8,128)} copy(f32[8,128,4,512]{1,0,3,2:T(8,128)} %broadcast_multiply_fusion) | data formatting | bytes 16777216 | tf_op jit(solution)/shard_map/mul | solution.py:169
  565.4 19.0 %bitcast_multiply_fusion = f32[4,512,512]{2,1,0:T(8,128)S(1)} fusion(f32[1024,4,512]{2,0,1:T(8,128)} %bitcast.134, f32[4,1024,512]{2,1,0:T(8,128)} %param.18, f32[4,512]{1,0:T(4,128)S(1)} %subtract_exponential_fusion.4, f32[4,512]{1,0:T(4,128)S(1)} %fusion.44, f32[1,512,512]{2,1,0:T(8,128)S(1)} %get-tuple-element.16, ...), kind=kOutput, calls=%fused_computation.11 | convolution fusion | flops 6448742400 | bytes 25182208 | tf_op jit(solution)/shard_map/uij,iub->ujb/dot_general | solution.py:170
  584.9 3.3 collective-permute-start.21
  588.2 1.4 collective-permute-start.18
  589.5 1.4 collective-permute-start.15
  590.9 1.6 collective-permute-start.12
  592.5 19.1 %collective-permute-done.21 = f32[512,512]{1,0:T(8,128)S(1)} collective-permute-done((f32[512,512]{1,0:T(8,128)S(1)}, f32[512,512]{1,0:T(8,128)S(1)}, u32[]{:S(2)}, u32[]{:S(2)}) %collective-permute-start.21) | collective-permute-done | bytes 1048608 | tf_op jit(solution)/shard_map/ppermute | solution.py:29
  611.6 22.5 %collective-permute-done.18 = f32[512,512]{1,0:T(8,128)S(1)} collective-permute-done((f32[512,512]{1,0:T(8,128)S(1)}, f32[512,512]{1,0:T(8,128)S(1)}, u32[]{:S(2)}, u32[]{:S(2)}) %collective-permute-start.18) | collective-permute-done | bytes 1048608 | tf_op jit(solution)/shard_map/ppermute | solution.py:29
  634.1 22.5 %collective-permute-done.15 = f32[512,512]{1,0:T(8,128)S(1)} collective-permute-done((f32[512,512]{1,0:T(8,128)S(1)}, f32[512,512]{1,0:T(8,128)S(1)}, u32[]{:S(2)}, u32[]{:S(2)}) %collective-permute-start.15) | collective-permute-done | bytes 1048608 | tf_op jit(solution)/shard_map/ppermute | solution.py:29
  656.5 21.8 %collective-permute-done.12 = f32[512,512]{1,0:T(8,128)S(1)} collective-permute-done((f32[512,512]{1,0:T(8,128)S(1)}, f32[512,512]{1,0:T(8,128)S(1)}, u32[]{:S(2)}, u32[]{:S(2)}) %collective-permute-start.12) | collective-permute-done | bytes 1048608 | tf_op jit(solution)/shard_map/ppermute | solution.py:29
  682.6 1.4 collective-permute-start.23
  684.2 1.3 collective-permute-start.20
  685.7 1.3 collective-permute-start.17
  687.3 1.3 collective-permute-start.14
  688.6 43.3 %collective-permute-done.23 = f32[512,512]{1,0:T(8,128)S(1)} collective-permute-done((f32[512,512]{1,0:T(8,128)S(1)}, f32[512,512]{1,0:T(8,128)S(1)}, u32[]{:S(2)}, u32[]{:S(2)}) %collective-permute-start.23) | collective-permute-done | bytes 1048608 | tf_op jit(solution)/shard_map/ppermute | solution.py:49
  731.8 22.5 %collective-permute-done.20 = f32[512,512]{1,0:T(8,128)S(1)} collective-permute-done((f32[512,512]{1,0:T(8,128)S(1)}, f32[512,512]{1,0:T(8,128)S(1)}, u32[]{:S(2)}, u32[]{:S(2)}) %collective-permute-start.20) | collective-permute-done | bytes 1048608 | tf_op jit(solution)/shard_map/ppermute | solution.py:49
  754.3 22.5 %collective-permute-done.17 = f32[512,512]{1,0:T(8,128)S(1)} collective-permute-done((f32[512,512]{1,0:T(8,128)S(1)}, f32[512,512]{1,0:T(8,128)S(1)}, u32[]{:S(2)}, u32[]{:S(2)}) %collective-permute-start.17) | collective-permute-done | bytes 1048608 | tf_op jit(solution)/shard_map/ppermute | solution.py:49
  776.8 22.4 %collective-permute-done.14 = f32[512,512]{1,0:T(8,128)S(1)} collective-permute-done((f32[512,512]{1,0:T(8,128)S(1)}, f32[512,512]{1,0:T(8,128)S(1)}, u32[]{:S(2)}, u32[]{:S(2)}) %collective-permute-start.14) | collective-permute-done | bytes 1048608 | tf_op jit(solution)/shard_map/ppermute | solution.py:49
  799.2 1.3 divide_bitcast_fusion.1
  800.5 1.5 pad_maximum_fusion.1
  802.6 12.9 %multiply_multiply_fusion.1 = f32[4,1024,512]{2,1,0:T(8,128)} fusion(f32[4,1024,512]{2,1,0:T(8,128)} %param.18, f32[1024,4,512]{2,0,1:T(8,128)} %bitcast.135, f32[4,512]{1,0:T(4,128)S(1)} %subtract_exponential_fusion.4, f32[4,512]{1,0:T(4,128)S(1)} %fusion.44, f32[1,512,512]{2,1,0:T(8,128)S(1)} %get-tuple-element.16, ...), kind=kOutput, calls=%fused_computation.5 | convolution fusion | flops 6451888128 | bytes 29376512 | tf_op jit(solution)/shard_map/iub,ujb->uij/dot_general | solution.py:174
  815.5 75.5 %all-gather.10.cloned.1.call-done = f32[4096,2,512]{2,0,1:T(8,128)} async-done(((f32[512,2,512]{2,0,1:T(8,128)}), f32[4096,2,512]{2,0,1:T(8,128)}) %all-gather.10.cloned.1.call-update) | async-done | bytes 16777232 | tf_op jit(solution)/shard_map/all_gather | solution.py:126
  891.0 23.5 %multiply_multiply_fusion = f32[2,4096,512]{2,1,0:T(8,128)} fusion(f32[2,4096,512]{2,1,0:T(8,128)} %param.17, f32[4096,2,512]{2,0,1:T(8,128)} %all-gather.10.cloned.1.call-done, f32[2,512,512]{2,1,0:T(8,128)} %copy-done.3), kind=kOutput, calls=%fused_computation | convolution fusion | flops 12893290496 | bytes 52428800 | tf_op jit(solution)/shard_map/igb,gjb->gij/dot_general | solution.py:128
  (75 shorter events, 17.1 us)
Async XLA Ops:
  7.2 281.9 %copy-start = (f32[4,512,256]{2,1,0:T(8,128)S(1)}, f32[4,512,256]{2,1,0:T(8,128)}, u32[]{:S(2)}) copy-start(f32[4,512,256]{2,1,0:T(8,128)} %param.15) | copy-start | bytes 6291460
  7.2 100.4 %reduce-scatter.6.cloned.1.call-start = ((), (), s32[]{:S(2)}) async-start(), calls=%async_computation.4 | async-start | bytes 9437184 | tf_op jit(solution)/shard_map/reduce_scatter | solution.py:92
  23.4 1.3 copy-start.3
  35.9 147.5 %reduce-scatter.4.cloned.1.call-start = ((), (), s32[]{:S(2)}) async-start(), calls=%async_computation.3 | async-start | bytes 9437184 | tf_op jit(solution)/shard_map/reduce_scatter | solution.py:92
  47.6 0.7 copy-start.10
  47.7 433.2 %reduce-scatter.8.cloned.1.call-start = ((), (), s32[]{:S(2)}) async-start(), calls=%async_computation.5 | async-start | bytes 9437184 | tf_op jit(solution)/shard_map/reduce_scatter | solution.py:148
  185.7 26.9 %collective-permute-start = (f32[512,512]{1,0:T(8,128)S(1)}, f32[512,512]{1,0:T(8,128)S(1)}, u32[]{:S(2)}, u32[]{:S(2)}) collective-permute-start(f32[512,512]{1,0:T(8,128)S(1)} %get-tuple-element.19), channel_id=1, source_target_pairs={{0,8},{24,16},{1,9},{25,17},{2,10},{26,18},{3,11},{27,19},{4,12},{... | collective-permute-start | bytes 3145736 | tf_op jit(solution)/shard_map/ppermute | solution.py:29
  189.1 46.0 %collective-permute-start.3 = (f32[512,512]{1,0:T(8,128)S(1)}, f32[512,512]{1,0:T(8,128)S(1)}, u32[]{:S(2)}, u32[]{:S(2)}) collective-permute-start(f32[512,512]{1,0:T(8,128)S(1)} %get-tuple-element.20), channel_id=1, source_target_pairs={{0,8},{24,16},{1,9},{25,17},{2,10},{26,18},{3,11},{27,19},{4,12},{... | collective-permute-start | bytes 3145736 | tf_op jit(solution)/shard_map/ppermute | solution.py:29
  190.5 67.1 %collective-permute-start.6 = (f32[512,512]{1,0:T(8,128)S(1)}, f32[512,512]{1,0:T(8,128)S(1)}, u32[]{:S(2)}, u32[]{:S(2)}) collective-permute-start(f32[512,512]{1,0:T(8,128)S(1)} %get-tuple-element.21), channel_id=1, source_target_pairs={{0,8},{24,16},{1,9},{25,17},{2,10},{26,18},{3,11},{27,19},{4,12},{... | collective-permute-start | bytes 3145736 | tf_op jit(solution)/shard_map/ppermute | solution.py:29
  191.8 87.0 %collective-permute-start.9 = (f32[512,512]{1,0:T(8,128)S(1)}, f32[512,512]{1,0:T(8,128)S(1)}, u32[]{:S(2)}, u32[]{:S(2)}) collective-permute-start(f32[512,512]{1,0:T(8,128)S(1)} %get-tuple-element.22), channel_id=1, source_target_pairs={{0,8},{24,16},{1,9},{25,17},{2,10},{26,18},{3,11},{27,19},{4,12},{... | collective-permute-start | bytes 3145736 | tf_op jit(solution)/shard_map/ppermute | solution.py:29
  212.8 67.0 %collective-permute-start.1 = (f32[512,512]{1,0:T(8,128)S(1)}, f32[512,512]{1,0:T(8,128)S(1)}, u32[]{:S(2)}, u32[]{:S(2)}) collective-permute-start(f32[512,512]{1,0:T(8,128)S(1)} %add.155), channel_id=1, source_target_pairs={{8,16},{16,8},{9,17},{17,9},{10,18},{18,10},{11,19},{19,11},{12,20... | collective-permute-start | bytes 3145736 | tf_op jit(solution)/shard_map/ppermute | solution.py:39
  235.3 46.2 %collective-permute-start.4 = (f32[512,512]{1,0:T(8,128)S(1)}, f32[512,512]{1,0:T(8,128)S(1)}, u32[]{:S(2)}, u32[]{:S(2)}) collective-permute-start(f32[512,512]{1,0:T(8,128)S(1)} %add.159), channel_id=1, source_target_pairs={{8,16},{16,8},{9,17},{17,9},{10,18},{18,10},{11,19},{19,11},{12,20... | collective-permute-start | bytes 3145736 | tf_op jit(solution)/shard_map/ppermute | solution.py:39
  257.7 26.3 %collective-permute-start.7 = (f32[512,512]{1,0:T(8,128)S(1)}, f32[512,512]{1,0:T(8,128)S(1)}, u32[]{:S(2)}, u32[]{:S(2)}) collective-permute-start(f32[512,512]{1,0:T(8,128)S(1)} %add.163), channel_id=1, source_target_pairs={{8,16},{16,8},{9,17},{17,9},{10,18},{18,10},{11,19},{19,11},{12,20... | collective-permute-start | bytes 3145736 | tf_op jit(solution)/shard_map/ppermute | solution.py:39
  279.1 7.5 collective-permute-start.10
  280.0 7.7 copy-start.4
  280.0 9.0 copy-start.8
  280.1 30.7 %collective-permute-start.2 = (f32[512,512]{1,0:T(8,128)S(1)}, f32[512,512]{1,0:T(8,128)}, u32[]{:S(2)}, u32[]{:S(2)}) collective-permute-start(f32[512,512]{1,0:T(8,128)S(1)} %add.156), channel_id=1, source_target_pairs={{8,0},{16,24},{9,1},{17,25},{10,2},{18,26},{11,3},{19,27},{12,4},{... | collective-permute-start | bytes 3145736 | tf_op jit(solution)/shard_map/ppermute | solution.py:49
  282.7 50.6 %collective-permute-start.5 = (f32[512,512]{1,0:T(8,128)}, f32[512,512]{1,0:T(8,128)}, u32[]{:S(2)}, u32[]{:S(2)}) collective-permute-start(f32[512,512]{1,0:T(8,128)} %add.160), channel_id=1, source_target_pairs={{8,0},{16,24},{9,1},{17,25},{10,2},{18,26},{11,3},{19,27},{12,4},{... | collective-permute-start | bytes 3145736 | tf_op jit(solution)/shard_map/ppermute | solution.py:49
  285.3 70.5 %collective-permute-start.8 = (f32[512,512]{1,0:T(8,128)}, f32[512,512]{1,0:T(8,128)}, u32[]{:S(2)}, u32[]{:S(2)}) collective-permute-start(f32[512,512]{1,0:T(8,128)} %add.164), channel_id=1, source_target_pairs={{8,0},{16,24},{9,1},{17,25},{10,2},{18,26},{11,3},{19,27},{12,4},{... | collective-permute-start | bytes 3145736 | tf_op jit(solution)/shard_map/ppermute | solution.py:49
  287.7 88.4 %collective-permute-start.11 = (f32[512,512]{1,0:T(8,128)}, f32[512,512]{1,0:T(8,128)}, u32[]{:S(2)}, u32[]{:S(2)}) collective-permute-start(f32[512,512]{1,0:T(8,128)} %add.168), channel_id=1, source_target_pairs={{8,0},{16,24},{9,1},{17,25},{10,2},{18,26},{11,3},{19,27},{12,4},{... | collective-permute-start | bytes 3145736 | tf_op jit(solution)/shard_map/ppermute | solution.py:49
  289.0 87.1 %copy-start.5 = (f32[512,512]{1,0:T(8,128)S(1)}, f32[512,512]{1,0:T(8,128)}, u32[]{:S(2)}) copy-start(f32[512,512]{1,0:T(8,128)} %copy-done.4) | copy-start | bytes 3145732
  379.9 1.0 copy-start.2
  411.2 73.0 %copy-start.9 = (s32[512]{0:T(512)S(1)}, s32[512]{0:T(512)}, u32[]{:S(2)}) copy-start(s32[512]{0:T(512)} %param.12) | copy-start | bytes 6148
  411.2 135.0 %all-gather.12.cloned.1.call-start = ((), (), s32[]{:S(2)}) async-start(), calls=%async_computation.7 | async-start | bytes 9437184 | tf_op jit(solution)/shard_map/all_gather | solution.py:160
  489.7 401.3 %all-gather.10.cloned.1.call-start = ((), (), s32[]{:S(2)}) async-start(), calls=%async_computation.6 | async-start | bytes 18874368 | tf_op jit(solution)/shard_map/all_gather | solution.py:126
  584.9 26.7 %collective-permute-start.21 = (f32[512,512]{1,0:T(8,128)S(1)}, f32[512,512]{1,0:T(8,128)S(1)}, u32[]{:S(2)}, u32[]{:S(2)}) collective-permute-start(f32[512,512]{1,0:T(8,128)S(1)} %get-tuple-element.11), channel_id=1, source_target_pairs={{0,8},{24,16},{1,9},{25,17},{2,10},{26,18},{3,11},{27,19},{4,12},{... | collective-permute-start | bytes 3145736 | tf_op jit(solution)/shard_map/ppermute | solution.py:29
  588.2 45.9 %collective-permute-start.18 = (f32[512,512]{1,0:T(8,128)S(1)}, f32[512,512]{1,0:T(8,128)S(1)}, u32[]{:S(2)}, u32[]{:S(2)}) collective-permute-start(f32[512,512]{1,0:T(8,128)S(1)} %get-tuple-element.12), channel_id=1, source_target_pairs={{0,8},{24,16},{1,9},{25,17},{2,10},{26,18},{3,11},{27,19},{4,12},{... | collective-permute-start | bytes 3145736 | tf_op jit(solution)/shard_map/ppermute | solution.py:29
  589.5 67.0 %collective-permute-start.15 = (f32[512,512]{1,0:T(8,128)S(1)}, f32[512,512]{1,0:T(8,128)S(1)}, u32[]{:S(2)}, u32[]{:S(2)}) collective-permute-start(f32[512,512]{1,0:T(8,128)S(1)} %get-tuple-element.13), channel_id=1, source_target_pairs={{0,8},{24,16},{1,9},{25,17},{2,10},{26,18},{3,11},{27,19},{4,12},{... | collective-permute-start | bytes 3145736 | tf_op jit(solution)/shard_map/ppermute | solution.py:29
  590.9 87.4 %collective-permute-start.12 = (f32[512,512]{1,0:T(8,128)S(1)}, f32[512,512]{1,0:T(8,128)S(1)}, u32[]{:S(2)}, u32[]{:S(2)}) collective-permute-start(f32[512,512]{1,0:T(8,128)S(1)} %get-tuple-element.14), channel_id=1, source_target_pairs={{0,8},{24,16},{1,9},{25,17},{2,10},{26,18},{3,11},{27,19},{4,12},{... | collective-permute-start | bytes 3145736 | tf_op jit(solution)/shard_map/ppermute | solution.py:29
  679.4 2.9 collective-permute-start.22
  680.1 3.9 collective-permute-start.19
  680.8 4.7 collective-permute-start.16
  681.6 5.5 collective-permute-start.13
  682.5 116.6 %copy-start.6 = (f32[512,512]{1,0:T(8,128)S(1)}, f32[512,512]{1,0:T(8,128)}, u32[]{:S(2)}) copy-start(f32[512,512]{1,0:T(8,128)} %reduce-scatter.6.cloned.1.call-done) | copy-start | bytes 3145732
  682.5 116.6 %copy-start.7 = (f32[512,512]{1,0:T(8,128)S(1)}, f32[512,512]{1,0:T(8,128)}, u32[]{:S(2)}) copy-start(f32[512,512]{1,0:T(8,128)} %reduce-scatter.4.cloned.1.call-done) | copy-start | bytes 3145732
  682.6 49.3 %collective-permute-start.23 = (f32[512,512]{1,0:T(8,128)S(1)}, f32[512,512]{1,0:T(8,128)S(1)}, u32[]{:S(2)}, u32[]{:S(2)}) collective-permute-start(f32[512,512]{1,0:T(8,128)S(1)} %add.184), channel_id=1, source_target_pairs={{8,0},{16,24},{9,1},{17,25},{10,2},{18,26},{11,3},{19,27},{12,4},{... | collective-permute-start | bytes 3145736 | tf_op jit(solution)/shard_map/ppermute | solution.py:49
  684.2 70.1 %collective-permute-start.20 = (f32[512,512]{1,0:T(8,128)S(1)}, f32[512,512]{1,0:T(8,128)S(1)}, u32[]{:S(2)}, u32[]{:S(2)}) collective-permute-start(f32[512,512]{1,0:T(8,128)S(1)} %add.181), channel_id=1, source_target_pairs={{8,0},{16,24},{9,1},{17,25},{10,2},{18,26},{11,3},{19,27},{12,4},{... | collective-permute-start | bytes 3145736 | tf_op jit(solution)/shard_map/ppermute | solution.py:49
  685.7 91.0 %collective-permute-start.17 = (f32[512,512]{1,0:T(8,128)S(1)}, f32[512,512]{1,0:T(8,128)S(1)}, u32[]{:S(2)}, u32[]{:S(2)}) collective-permute-start(f32[512,512]{1,0:T(8,128)S(1)} %add.178), channel_id=1, source_target_pairs={{8,0},{16,24},{9,1},{17,25},{10,2},{18,26},{11,3},{19,27},{12,4},{... | collective-permute-start | bytes 3145736 | tf_op jit(solution)/shard_map/ppermute | solution.py:49
  687.3 111.9 %collective-permute-start.14 = (f32[512,512]{1,0:T(8,128)S(1)}, f32[512,512]{1,0:T(8,128)S(1)}, u32[]{:S(2)}, u32[]{:S(2)}) collective-permute-start(f32[512,512]{1,0:T(8,128)S(1)} %add.176), channel_id=1, source_target_pairs={{8,0},{16,24},{9,1},{17,25},{10,2},{18,26},{11,3},{19,27},{12,4},{... | collective-permute-start | bytes 3145736 | tf_op jit(solution)/shard_map/ppermute | solution.py:49
  891.0 23.5 %copy-start.1 = (f32[4,512,256]{2,1,0:T(8,128)S(1)}, f32[4,512,256]{2,1,0:T(8,128)}, u32[]{:S(2)}) copy-start(f32[4,512,256]{2,1,0:T(8,128)} %param.15) | copy-start | bytes 6291460
Sparse Core Ops, SparseCore 0:
  36.0 71.5 reduce-scatter.5
  112.0 71.2 reduce-scatter.3
  411.3 69.4 reduce-scatter.7
  489.8 56.3 all-gather.11
  802.1 88.8 all-gather.9
